TPU v7x, 32 devices: a whole 2x2x4 slice. The times are simulated.
32 devices in a mesh: graph: 8 (over z, y), leaf: 4 (over x, core).
Axes of the slice: x: 2, y: 2, z: 4, core: 2. Of those that a mesh axis runs over, the one named last changes fastest.
Arguments:
- weights: float32 [2, 1171200], P(None, ('graph', 'leaf'))
- first_moment: float32 [2, 1171200], P(None, ('graph', 'leaf'))
- second_moment: float32 [2, 1171200], P(None, ('graph', 'leaf'))
- centers: bfloat16 [8, 80, 300], P('graph'), may hold values from -6 to 6
- leaves: bfloat16 [8, 4096, 300], P('graph', 'leaf'), may hold values from -6 to 6
- edge_feats: bfloat16 [8, 4096, 300], P('graph', 'leaf'), may hold values from -6 to 6
- center_cot: bfloat16 [8, 80, 300], P('graph'), may hold values from -6 to 6
- leaf_cot: bfloat16 [8, 4096, 300], P('graph', 'leaf'), may hold values from -6 to 6
- edge_cot: bfloat16 [8, 4096, 300], P('graph', 'leaf'), may hold values from -6 to 6
- graph_ids: int32 [8, 4096], P('graph', 'leaf'), may hold values from 0 to 79, never falling along the last dimension, each value on 1 to 100 neighbouring positions
- star_sizes: int32 [8, 80], P('graph'), may hold values from 5 to 100
- leaf_mask: int32 [8, 4096], P('graph', 'leaf'), may hold values 0 or 1
- owner_list: int32 [32], replicated, may hold values from 0 to 31, as said below
Outputs:
- centers_out: bfloat16 [8, 80, 300], P('graph')
- leaves_out: bfloat16 [8, 4096, 300], P('graph', 'leaf')
- edges_out: bfloat16 [8, 4096, 300], P('graph', 'leaf')
- grad_centers: float32 [8, 80, 300], P('graph')
- grad_leaves: float32 [8, 4096, 300], P('graph', 'leaf')
- grad_edges: float32 [8, 4096, 300], P('graph', 'leaf')
- first_new: float32 [2, 1171200], P(None, ('graph', 'leaf'))
- second_new: float32 [2, 1171200], P(None, ('graph', 'leaf'))
- weights_new: float32 [2, 1171200], P(None, ('graph', 'leaf'))
- weights_low: bfloat16 [2, 1171200], P(None, ('graph', 'leaf'))
- weight_grads: float32 [2, 1171200], P(None, ('graph', 'leaf'))
Inputs may be any that keep to these rules, and one draw needn't show every extreme that they name: `graph_ids`: star numbers never fall along a group's slots; each star has 1 to 100 slots, one exactly 100. `owner_list`: a permutation of the holders.
All inputs are finite; a program needn't handle non-finite values. No bound on the sum of `leaf_mask` on one device may be relied on, other than what follows from the above.
Results may differ from a plain program's by a relative error of at most 0.04.
Values may be sent and summed in bfloat16 or wider, within the bound.
No kernel may reach another device: no remote copies, remote signals or barrier semaphores. Data moves between devices by JAX's collectives and lax.ppermute only.
A program may use at most 192 MiB of HBM per device.

v0:
```python
import math

import jax
import jax.numpy as jnp
from jax import lax
from jax.sharding import PartitionSpec as P

D = 300
HEADS = 12
HEAD = 25
FF = 1200
LAYERS = 2
STEP = 5


NEG = -1e30
EPS_NORM = 1e-05
BETA_ONE = 0.9
BETA_TWO = 0.999
RATE = 0.05
DECAY = 0.01
EPS_ADAM = 1e-08
INV_ROOT_TWO = 0.7071067811865476
INV_ROOT_TWO_PI = 0.3989422804014327


def joined_2(x, axis, join):
    gathered = jax.tree.map(
        lambda a, kind: lax.all_gather(a.astype(kind), axis),
        x,
        (jnp.bfloat16, jnp.bfloat16, jnp.bfloat16),
    )

    def take(source):
        return jax.tree.map(
            lambda a, own: lax.dynamic_index_in_dim(a, source, 0, False).astype(own.dtype),
            gathered,
            x,
        )

    return lax.fori_loop(
        1, lax.axis_size(axis), lambda source, state: join(state, take(source)), take(0)
    )


def split_params(flat_vec, model_width, hidden_width):
    square = model_width * model_width
    matrices = [
        flat_vec[i * square : (i + 1) * square].reshape(model_width, model_width) for i in range(5)
    ]
    offset = 5 * square
    w_one = flat_vec[offset : offset + model_width * hidden_width].reshape(
        model_width, hidden_width
    )
    offset = offset + model_width * hidden_width
    w_two = flat_vec[offset : offset + hidden_width * model_width].reshape(
        hidden_width, model_width
    )
    offset = offset + hidden_width * model_width
    norm_rows = flat_vec[offset : offset + 4 * model_width].reshape(4, model_width)
    return matrices + [w_one, w_two, norm_rows]


def matmul(left, right):
    return jnp.dot(left, right, preferred_element_type=jnp.float32)


def back_dot(grad_in, matrix):
    return lax.dot_general(
        grad_in, matrix, (((1,), (1,)), ((), ())), preferred_element_type=jnp.float32
    )


def contract(left, right):
    return lax.dot_general(
        left, right, (((0,), (0,)), ((), ())), preferred_element_type=jnp.float32
    )


def star_sum(onehot, values):
    return lax.dot_general(
        onehot,
        values,
        (((0,), (0,)), ((), ())),
        precision=lax.Precision.HIGHEST,
        preferred_element_type=jnp.float32,
    )


def head_table():
    feature_head = jnp.arange(D, dtype=jnp.int32) // HEAD
    return (feature_head[None, :] == jnp.arange(HEADS, dtype=jnp.int32)[:, None]).astype(
        jnp.float32
    )


def head_sum(values):
    return lax.dot_general(
        values,
        head_table(),
        (((1,), (1,)), ((), ())),
        precision=lax.Precision.HIGHEST,
        preferred_element_type=jnp.float32,
    )


def spread(values):
    return jnp.dot(
        values, head_table(), precision=lax.Precision.HIGHEST, preferred_element_type=jnp.float32
    )


def gelu_value(inputs):
    return inputs * (0.5 * (1.0 + lax.erf(inputs * INV_ROOT_TWO)))


def gelu_slope(inputs):
    cumulative = 0.5 * (1.0 + lax.erf(inputs * INV_ROOT_TWO))
    return cumulative + inputs * jnp.exp(-0.5 * inputs * inputs) * INV_ROOT_TWO_PI


def normalize(inputs, gain_row, shift_row):
    center_mean = jnp.mean(inputs, axis=-1, keepdims=True)
    deviation = inputs - center_mean
    variance = jnp.mean(deviation * deviation, axis=-1, keepdims=True)
    inverse = lax.rsqrt(variance + EPS_NORM)
    scaled = deviation * inverse
    return (scaled * gain_row + shift_row, scaled, inverse)


def norm_back(grad_out, gain_row, scaled, inverse):
    grad_scaled = grad_out * gain_row
    mean_one = jnp.mean(grad_scaled, axis=-1, keepdims=True)
    mean_two = jnp.mean(grad_scaled * scaled, axis=-1, keepdims=True)
    return inverse * (grad_scaled - mean_one - scaled * mean_two)


def combine(first, second):
    top_score = jnp.maximum(first[0], second[0])
    factor_a = jnp.exp(first[0] - top_score)
    factor_b = jnp.exp(second[0] - top_score)
    return (
        top_score,
        first[1] * spread(factor_a) + second[1] * spread(factor_b),
        first[2] * factor_a + second[2] * factor_b,
    )


def forward_layer(params, carried, structure, again):
    w_query, w_key, w_value, w_out, w_edge, w_one, w_two, norm_rows = params
    onehot, live_mask, star_scale, star_ids, center_flag = structure
    center_in, leaf_in, edge_in = carried
    star_count = center_in.shape[0]
    edge_low = edge_in.astype(jnp.bfloat16)
    edge_wide = edge_low.astype(jnp.float32)
    edge_next = matmul(edge_low, w_edge)
    message = (leaf_in * edge_wide).astype(jnp.bfloat16)
    center_low = center_in.astype(jnp.bfloat16)
    keys = matmul(message, w_key)
    values = matmul(message, w_value)
    query = matmul(center_low, w_query)
    self_key = matmul(center_low, w_key)
    self_value = matmul(center_low, w_value)
    center_rows = jnp.take(center_in, star_ids, axis=0)
    leaf_message = (center_rows * edge_wide).astype(jnp.bfloat16)
    leaf_out = matmul(leaf_message, w_value)
    scale_rows = jnp.take(star_scale, star_ids)
    scores = scale_rows[:, None] * head_sum(jnp.take(query, star_ids, axis=0) * keys)
    self_scores = star_scale[:, None] * head_sum(query * self_key)
    member = onehot[:, :, None] * live_mask[:, None, None] > 0.5
    local_max = jnp.max(jnp.where(member, scores[:, None, :], NEG), axis=0)
    shifted = jnp.where(
        live_mask[:, None] > 0.5, scores - jnp.take(local_max, star_ids, axis=0), NEG
    )
    weights_leaf = jnp.exp(shifted)
    numerator = star_sum(onehot, spread(weights_leaf) * values)
    denominator = star_sum(onehot, weights_leaf)
    if again:
        merged_max, merged_num, merged_den = joined_2(
            (local_max, numerator, denominator), "leaf", combine
        )
    else:
        merged_max, merged_num, merged_den = joined_2(
            (local_max, numerator, denominator), "leaf", combine
        )
    total_max = jnp.maximum(merged_max, self_scores)
    old_factor = jnp.exp(merged_max - total_max)
    self_weight = jnp.exp(self_scores - total_max)
    denom_all = merged_den * old_factor + self_weight
    numer_all = merged_num * spread(old_factor) + spread(self_weight) * self_value
    attended = numer_all / spread(denom_all)
    log_total = total_max + jnp.log(denom_all)
    attn_center = matmul(attended.astype(jnp.bfloat16), w_out)
    attn_leaf = matmul(leaf_out.astype(jnp.bfloat16), w_out)
    joined = jnp.concatenate([center_in + attn_center, leaf_in + attn_leaf], axis=0)
    norm_wide = norm_rows.astype(jnp.float32)
    normed, scaled_one, inverse_one = normalize(joined, norm_wide[0], norm_wide[1])
    normed_low = normed.astype(jnp.bfloat16)
    hidden_pre = matmul(normed_low, w_one)
    active_low = gelu_value(hidden_pre).astype(jnp.bfloat16)
    branch = matmul(active_low, w_two)
    output, scaled_two, inverse_two = normalize(normed + branch, norm_wide[2], norm_wide[3])
    saved_acts = (
        center_in,
        leaf_in,
        edge_low,
        message,
        leaf_message,
        center_low,
        query,
        keys,
        values,
        self_key,
        self_value,
        leaf_out,
        attended,
        log_total,
        self_scores,
        normed_low,
        scaled_one,
        inverse_one,
        hidden_pre,
        active_low,
        scaled_two,
        inverse_two,
    )
    return ((output[:star_count], output[star_count:], edge_next), saved_acts)


def backward_layer(params, saved_acts, upstream, structure):
    w_query, w_key, w_value, w_out, w_edge, w_one, w_two, norm_rows = params
    onehot, live_mask, star_scale, star_ids, center_flag = structure
    (
        center_in,
        leaf_in,
        edge_low,
        message,
        leaf_message,
        center_low,
        query,
        keys,
        values,
        self_key,
        self_value,
        leaf_out,
        attended,
        log_total,
        self_scores,
        normed_low,
        scaled_one,
        inverse_one,
        hidden_pre,
        active_low,
        scaled_two,
        inverse_two,
    ) = saved_acts
    grad_center, grad_leaf, grad_edge = upstream
    star_count = center_in.shape[0]
    norm_wide = norm_rows.astype(jnp.float32)
    row_weight = jnp.concatenate(
        [
            center_flag * jnp.ones((star_count,), jnp.float32),
            jnp.ones((leaf_in.shape[0],), jnp.float32),
        ]
    )[:, None]
    row_low = row_weight.astype(jnp.bfloat16)
    grad_out = jnp.concatenate([grad_center, grad_leaf], axis=0)
    gain_two_grad = jnp.sum(row_weight * grad_out * scaled_two, axis=0)
    shift_two_grad = jnp.sum(row_weight * grad_out, axis=0)
    grad_mid = norm_back(grad_out, norm_wide[2], scaled_two, inverse_two)
    grad_branch = grad_mid.astype(jnp.bfloat16)
    w_two_grad = contract(active_low * row_low, grad_branch)
    grad_active = back_dot(grad_branch, w_two)
    grad_pre = (grad_active * gelu_slope(hidden_pre)).astype(jnp.bfloat16)
    w_one_grad = contract(normed_low * row_low, grad_pre)
    grad_normed = grad_mid + back_dot(grad_pre, w_one)
    gain_one_grad = jnp.sum(row_weight * grad_normed * scaled_one, axis=0)
    shift_one_grad = jnp.sum(row_weight * grad_normed, axis=0)
    grad_joined = norm_back(grad_normed, norm_wide[0], scaled_one, inverse_one)
    grad_attn_center = grad_joined[:star_count].astype(jnp.bfloat16)
    grad_attn_leaf = grad_joined[star_count:].astype(jnp.bfloat16)
    w_out_grad = center_flag * contract(attended.astype(jnp.bfloat16), grad_attn_center) + contract(
        leaf_out.astype(jnp.bfloat16), grad_attn_leaf
    )
    grad_attended = back_dot(grad_attn_center, w_out)
    grad_leaf_out = back_dot(grad_attn_leaf, w_out).astype(jnp.bfloat16)
    grad_leaf_msg = back_dot(grad_leaf_out, w_value)
    edge_wide = edge_low.astype(jnp.float32)
    center_rows = jnp.take(center_in, star_ids, axis=0)
    center_part = star_sum(onehot, grad_leaf_msg * edge_wide)
    edge_grad_acc = grad_leaf_msg * center_rows
    scale_rows = jnp.take(star_scale, star_ids)
    query_rows = jnp.take(query, star_ids, axis=0)
    scores = scale_rows[:, None] * head_sum(query_rows * keys)
    probabilities = jnp.exp(
        jnp.where(live_mask[:, None] > 0.5, scores - jnp.take(log_total, star_ids, axis=0), NEG)
    )
    self_prob = jnp.exp(self_scores - log_total)
    grad_att_rows = jnp.take(grad_attended, star_ids, axis=0)
    delta_sum = head_sum(grad_attended * attended)
    grad_values = spread(probabilities) * grad_att_rows
    grad_self_value = (spread(self_prob) * grad_attended).astype(jnp.bfloat16)
    grad_scores = probabilities * (
        head_sum(grad_att_rows * values) - jnp.take(delta_sum, star_ids, axis=0)
    )
    grad_self_scores = self_prob * (head_sum(grad_attended * self_value) - delta_sum)
    leaf_coef = spread(grad_scores * scale_rows[:, None])
    query_part = star_sum(onehot, leaf_coef * keys)
    grad_keys = (leaf_coef * query_rows).astype(jnp.bfloat16)
    self_coef = spread(grad_self_scores * star_scale[:, None])
    summed_query, summed_center = (
        lax.psum(query_part.astype(jnp.bfloat16), "leaf").astype(jnp.float32),
        lax.psum(center_part.astype(jnp.bfloat16), "leaf").astype(jnp.float32),
    )
    grad_query = (summed_query + self_coef * self_key).astype(jnp.bfloat16)
    grad_self_key = (self_coef * query).astype(jnp.bfloat16)
    grad_values_low = grad_values.astype(jnp.bfloat16)
    w_query_grad = center_flag * contract(center_low, grad_query)
    w_key_grad = contract(message, grad_keys) + center_flag * contract(center_low, grad_self_key)
    w_value_grad = (
        contract(leaf_message, grad_leaf_out)
        + contract(message, grad_values_low)
        + center_flag * contract(center_low, grad_self_value)
    )
    grad_center_low = (
        back_dot(grad_query, w_query)
        + back_dot(grad_self_key, w_key)
        + back_dot(grad_self_value, w_value)
    )
    grad_message = back_dot(grad_keys, w_key) + back_dot(grad_values_low, w_value)
    grad_leaves = grad_joined[star_count:] + grad_message * edge_wide
    edge_grad_acc = edge_grad_acc + grad_message * leaf_in
    grad_next_low = grad_edge.astype(jnp.bfloat16)
    w_edge_grad = contract(edge_low, grad_next_low)
    grad_edges = edge_grad_acc + back_dot(grad_next_low, w_edge)
    grad_centers = grad_joined[:star_count] + grad_center_low + summed_center
    norm_grads = jnp.stack([gain_one_grad, shift_one_grad, gain_two_grad, shift_two_grad])
    grad_vec = jnp.concatenate(
        [
            w_query_grad.reshape(-1),
            w_key_grad.reshape(-1),
            w_value_grad.reshape(-1),
            w_out_grad.reshape(-1),
            w_edge_grad.reshape(-1),
            w_one_grad.reshape(-1),
            w_two_grad.reshape(-1),
            norm_grads.reshape(-1),
        ]
    )
    return ((grad_centers, grad_leaves, grad_edges), grad_vec)


def local(
    weights,
    first_moment,
    second_moment,
    centers,
    leaves,
    edge_feats,
    center_cot,
    leaf_cot,
    edge_cot,
    graph_ids,
    star_sizes,
    leaf_mask,
    owner_list,
):
    holders = lax.axis_size(("graph", "leaf"))
    block_len = weights.shape[1]
    gathered = lax.all_gather(weights.astype(jnp.bfloat16), ("graph", "leaf"), axis=1, tiled=True)
    ordered = jnp.take(gathered.reshape(LAYERS, holders, block_len), owner_list, axis=1).reshape(
        LAYERS, -1
    )
    layer_params = [split_params(ordered[i], D, FF) for i in range(LAYERS)]
    star_ids = graph_ids[0]
    star_count = centers.shape[1]
    onehot = (star_ids[:, None] == jnp.arange(star_count, dtype=jnp.int32)[None, :]).astype(
        jnp.float32
    )
    live_mask = leaf_mask[0].astype(jnp.float32)
    star_scale = jnp.log(star_sizes[0].astype(jnp.float32)) / (math.log(32.0) * math.sqrt(HEAD))
    center_flag = (lax.axis_index("leaf") == 0).astype(jnp.float32)
    structure = (onehot, live_mask, star_scale, star_ids, center_flag)
    carried = (
        centers[0].astype(jnp.float32),
        leaves[0].astype(jnp.float32),
        edge_feats[0].astype(jnp.float32),
    )
    layer_inputs = []
    stash_list = []
    for i in range(LAYERS):
        layer_inputs.append(carried)
        carried, saved_acts = forward_layer(layer_params[i], carried, structure, False)
        stash_list.append(saved_acts)
    upstream = (
        center_cot[0].astype(jnp.float32),
        leaf_cot[0].astype(jnp.float32),
        edge_cot[0].astype(jnp.float32),
    )
    flat_grads = [None] * LAYERS
    for i in reversed(range(LAYERS)):
        unused_out, saved_acts = forward_layer(layer_params[i], layer_inputs[i], structure, True)
        upstream, grad_vec = backward_layer(layer_params[i], saved_acts, upstream, structure)
        holder_vec = (
            jnp.zeros((holders, block_len), jnp.float32)
            .at[owner_list]
            .set(grad_vec.reshape(holders, block_len))
            .reshape(-1)
        )
        flat_grads[i] = holder_vec
    grad_total = lax.psum_scatter(
        jnp.stack(flat_grads), ("graph", "leaf"), scatter_dimension=1, tiled=True
    )
    first_new = BETA_ONE * first_moment + (1.0 - BETA_ONE) * grad_total
    second_new = BETA_TWO * second_moment + (1.0 - BETA_TWO) * grad_total * grad_total
    step_one = first_new / (1.0 - BETA_ONE**STEP)
    step_two = second_new / (1.0 - BETA_TWO**STEP)
    weights_new = weights - RATE * (step_one / (jnp.sqrt(step_two) + EPS_ADAM) + DECAY * weights)
    return (
        carried[0].astype(jnp.bfloat16)[None],
        carried[1].astype(jnp.bfloat16)[None],
        carried[2].astype(jnp.bfloat16)[None],
        upstream[0][None],
        upstream[1][None],
        upstream[2][None],
        first_new,
        second_new,
        weights_new,
        weights_new.astype(jnp.bfloat16),
        grad_total,
    )


def solution(mesh):
    return jax.shard_map(
        local,
        mesh=mesh,
        in_specs=(
            P(None, ("graph", "leaf")),
            P(None, ("graph", "leaf")),
            P(None, ("graph", "leaf")),
            P("graph", None, None),
            P("graph", "leaf", None),
            P("graph", "leaf", None),
            P("graph", None, None),
            P("graph", "leaf", None),
            P("graph", "leaf", None),
            P("graph", "leaf"),
            P("graph", None),
            P("graph", "leaf"),
            P(),
        ),
        out_specs=(
            P("graph", None, None),
            P("graph", "leaf", None),
            P("graph", "leaf", None),
            P("graph", None, None),
            P("graph", "leaf", None),
            P("graph", "leaf", None),
            P(None, ("graph", "leaf")),
            P(None, ("graph", "leaf")),
            P(None, ("graph", "leaf")),
            P(None, ("graph", "leaf")),
            P(None, ("graph", "leaf")),
        ),
        check_vma=False,
    )
```

profile of v0, /device:TPU:0, one launch (start us, length us, event | category | flops | bytes accessed | tf_op | source)
XLA Modules:
  0.0 954.7 jit_solution(16459822666604553747)
XLA Ops:
  10.5 6.6 gather_fusion.1
  30.1 47.8 %all-gather.13.cloned.1.call-done = bf16[32,36600,2]{1,2,0:T(2,128)(2,1)} async-done(((bf16[1,36600,2]{1,2,0:T(2,128)(2,1)}), bf16[32,36600,2]{1,2,0:T(2,128)(2,1)}) %all-gather.13.cloned.1.call-update) | async-done | bytes 4684816 | tf_op jit(solution)/shard_map/all_gather | solution.py:370
  78.0 4.9 copy.327
  82.9 11.8 %reshape.657 = bf16[2342400]{0:T(1024)(128)(2,1)} reshape(bf16[2,32,36600]{2,1,0:T(8,128)(2,1)} %bitcast.236) | data formatting | bytes 9369600
  94.7 11.3 %reshape.658 = bf16[2,1171200]{1,0:T(2,128)(2,1)} reshape(bf16[2342400]{0:T(1024)(128)(2,1)} %reshape.657) | data formatting | bytes 9369600
  106.0 5.5 bitcast_bitcast_fusion
  111.5 12.4 %reshape.659 = bf16[2342400]{0:T(1024)(128)(2,1)} reshape(bf16[2,1171200]{1,0:T(2,128)(2,1)} %bitcast_bitcast_fusion) | data formatting | bytes 9369600
  124.0 11.8 %reshape.391 = bf16[2,32,36600]{2,1,0:T(8,128)(2,1)} reshape(bf16[2342400]{0:T(1024)(128)(2,1)} %reshape.659) | data formatting | bytes 9369600 | tf_op jit(solution)/shard_map/reshape | solution.py:371
  135.8 9.3 copy.255
  145.1 13.7 %gather_fusion = bf16[32,2,36600]{2,1,0:T(2,128)(2,1)} fusion(bf16[2,32,36600]{2,0,1:T(2,128)(2,1)} %copy.255, s32[1024]{0:T(1024)S(1)} %pad_clamp_fusion), kind=kCustom, calls=%fused_computation.13 | custom fusion | bytes 9369728 | tf_op jit(solution)/shard_map/jit(_take)/gather | solution.py:371
  158.8 8.6 fusion.34
  167.4 49.0 %slice_reduce_fusion.1 = (bf16[32,36600]{1,0:T(8,128)(2,1)}, bf16[32,36600]{1,0:T(8,128)(2,1)S(1)}) fusion(bf16[2,32,36600]{2,0,1:T(2,128)(2,1)} %fusion.34), kind=kLoop, calls=%fused_computation.81 | loop fusion | bytes 9369600 | tf_op jit(solution)/shard_map/slice | solution.py:374
  216.3 8.2 slice.149
  231.1 4.8 gather_fusion.2
  245.9 7.3 slice.157
  258.8 5.3 all-gather.8
  266.8 6.0 all-gather.1
  272.8 5.2 all-gather.7
  277.9 4.6 while.56
  290.7 6.0 multiply_convert_fusion.1
  302.2 6.4 slice.164
  315.1 4.8 gather_fusion.7
  328.6 4.7 gather_fusion.5
  341.1 7.7 slice.174
  355.7 5.2 all-gather.10
  363.8 5.7 all-gather.4
  369.5 5.2 all-gather.9
  374.7 6.4 while.57
  398.8 5.1 fusion.24
  403.9 4.1 multiply_reduce_fusion
  412.2 4.8 gather_fusion.9
  417.2 5.9 fusion.35
  468.3 4.4 gather_fusion.11
  502.7 5.2 fusion.37
  508.0 6.3 fusion.25
  514.3 5.3 multiply_reduce_fusion.2
  528.5 4.8 gather_fusion.12
  553.5 4.0 gather_fusion.13
  587.8 46.3 %concatenate.34 = f32[1171200]{0:T(1024)} concatenate(f32[90000]{0:T(1024)} %reshape.401, f32[90000]{0:T(1024)} %reshape.402, f32[90000]{0:T(1024)} %reshape.403, f32[90000]{0:T(1024)} %reshape.404, f32[90000]{0:T(1024)} %reshape.405, f32[360000]{0:T(1024)} %reshape.406, f32[360000]{0:T(1024)} %reshape.407, f32[1200]{0:T(1024)S(1)} %reshape.408), dimensions={0} | concatenate | bytes 9369600 | tf_op jit(solution)/shard_map/concatenate | solution.py:338
  634.1 7.5 reshape.547
  641.5 7.6 scatter_custom_fusion.1
  649.2 12.4 %stack_reshape.7 = f32[1,1171200]{1,0:T(1,128)} reshape(f32[32,36600]{1,0:T(8,128)} %scatter_custom_fusion.1) | data formatting | bytes 9369600 | tf_op jit(solution)/shard_map/stack;reshape | solution.py:412
  673.8 41.1 %concatenate.33 = f32[1171200]{0:T(1024)} concatenate(f32[90000]{0:T(1024)} %reshape.392, f32[90000]{0:T(1024)S(1)} %copy-done.69, f32[90000]{0:T(1024)} %reshape.394, f32[90000]{0:T(1024)} %reshape.395, f32[90000]{0:T(1024)} %reshape.396, f32[360000]{0:T(1024)} %reshape.397, f32[360000]{0:T(1024)S(1)} %copy-done.44, f32[1200]{0:T(1024)S(1)} %reshape.399), dimensions={0} | concatenate | bytes 9369600 | tf_op jit(solution)/shard_map/concatenate | solution.py:338
  715.0 7.5 reshape.539
  722.4 7.4 scatter_custom_fusion
  729.9 12.3 %stack_reshape.6 = f32[1,1171200]{1,0:T(1,128)} reshape(f32[32,36600]{1,0:T(8,128)} %scatter_custom_fusion) | data formatting | bytes 9369600 | tf_op jit(solution)/shard_map/stack;reshape | solution.py:412
  742.1 11.1 %pad_maximum_fusion = f32[2,1171200]{1,0:T(2,128)} fusion(f32[1,1171200]{1,0:T(1,128)} %stack_reshape.7, f32[1,1171200]{1,0:T(1,128)} %stack_reshape.6), kind=kLoop, calls=%fused_computation.63 | loop fusion | flops 2342400 | bytes 18739200 | tf_op jit(solution)/shard_map/stack | solution.py:412
  782.2 162.7 %all-reduce.8.cloned.1.call-done = f32[2,1171200]{1,0:T(2,128)} async-done(((f32[2,1171200]{1,0:T(2,128)}), f32[2,1171200]{1,0:T(2,128)}) %all-reduce.8.cloned.1.call-update) | async-done | bytes 9369616
  (580 shorter events, 297.1 us)
Async XLA Ops:
  7.2 446.8 %copy-start = (bf16[1,1024,300]{1,2,0:T(8,128)(2,1)S(1)}, bf16[1,1024,300]{1,2,0:T(8,128)(2,1)}, u32[]{:S(2)}) copy-start(bf16[1,1024,300]{1,2,0:T(8,128)(2,1)} %param.31) | copy-start | bytes 1843204
  7.2 70.8 %all-gather.13.cloned.1.call-start = ((), (), s32[]{:S(2)}) async-start(), calls=%async_computation | async-start | bytes 4832256 | tf_op jit(solution)/shard_map/all_gather | solution.py:370
  9.0 485.5 %all-reduce.12.cloned.1.call-start = ((), (), s32[]{:S(2)}) async-start(), calls=%async_computation.3 | async-start | bytes 245760 | tf_op jit(solution)/shard_map/psum | solution.py:312
  10.5 6.6 copy-start.58
  20.6 6.8 copy-start.22
  23.5 6.7 copy-start.26
  27.3 333.7 %copy-start.115 = (pred[1024]{0:T(1024)(128)(4,1)}, pred[1024]{0:T(1024)(128)(4,1)S(1)}, u32[]{:S(2)}) copy-start(pred[1024]{0:T(1024)(128)(4,1)S(1)} %broadcast_compare_fusion) | copy-start | bytes 3076
  27.4 213.8 %copy-start.78 = (pred[1024,80]{0,1:T(8,128)(4,1)}, pred[1024,80]{0,1:T(8,128)(4,1)S(1)}, u32[]{:S(2)}) copy-start(pred[1024,80]{0,1:T(8,128)(4,1)S(1)} %select_compare_fusion) | copy-start | bytes 245764
  216.3 85.8 %copy-start.9 = (bf16[32,36600]{1,0:T(8,128)(2,1)}, bf16[32,36600]{1,0:T(8,128)(2,1)S(1)}, u32[]{:S(2)}) copy-start(bf16[32,36600]{1,0:T(8,128)(2,1)S(1)} %get-tuple-element.623) | copy-start | bytes 7027204
  241.1 22.9 %copy-start.63 = (f32[1024,12]{0,1:T(8,128)}, f32[1024,12]{0,1:T(8,128)S(1)}, u32[]{:S(2)}) copy-start(f32[1024,12]{0,1:T(8,128)S(1)} %fusion.110) | copy-start | bytes 147460
  244.6 40.0 %copy-start.71 = (f32[80,300]{1,0:T(8,128)}, f32[80,300]{1,0:T(8,128)S(1)}, u32[]{:S(2)}) copy-start(f32[80,300]{1,0:T(8,128)S(1)} %convolution_bitcast_fusion.1) | copy-start | bytes 288004
  286.4 10.3 %copy-start.74 = (f32[80,300]{1,0:T(8,128)}, f32[80,300]{1,0:T(8,128)S(1)}, u32[]{:S(2)}) copy-start(f32[80,300]{1,0:T(8,128)S(1)} %convolution_add_fusion.18) | copy-start | bytes 288004
  289.9 6.9 copy-start.5
  290.2 6.6 copy-start.104
  290.7 17.8 %copy-start.127 = (f32[300]{0:T(512)}, f32[300]{0:T(512)S(1)}, u32[]{:S(2)}) copy-start(f32[300]{0:T(512)S(1)} %get-tuple-element.644) | copy-start | bytes 3604
  300.5 8.0 copy-start.98
  323.3 62.1 %copy-start.38 = (bf16[1024,300]{1,0:T(8,128)(2,1)}, bf16[1024,300]{1,0:T(8,128)(2,1)S(1)}, u32[]{:S(2)}) copy-start(bf16[1024,300]{1,0:T(8,128)(2,1)S(1)} %get-tuple-element.693) | copy-start | bytes 1843204
  338.6 22.3 %copy-start.65 = (f32[1024,12]{0,1:T(8,128)}, f32[1024,12]{0,1:T(8,128)S(1)}, u32[]{:S(2)}) copy-start(f32[1024,12]{0,1:T(8,128)S(1)} %fusion.113) | copy-start | bytes 147460
  361.0 8.6 copy-start.129
  384.2 25.7 %copy-start.89 = (f32[80,300]{1,0:T(8,128)}, f32[80,300]{1,0:T(8,128)S(1)}, u32[]{:S(2)}) copy-start(f32[80,300]{1,0:T(8,128)S(1)} %convolution_divide_fusion) | copy-start | bytes 288004
  385.4 22.6 %copy-start.76 = (f32[80,300]{1,0:T(8,128)}, f32[80,300]{1,0:T(8,128)S(1)}, u32[]{:S(2)}) copy-start(f32[80,300]{1,0:T(8,128)S(1)} %convolution_add_fusion.17) | copy-start | bytes 288004
  387.8 20.2 %copy-start.7 = (f32[1024,300]{1,0:T(8,128)}, f32[1024,300]{1,0:T(8,128)S(1)}, u32[]{:S(2)}) copy-start(f32[1024,300]{1,0:T(8,128)S(1)} %convolution_add_fusion.6) | copy-start | bytes 3686404
  388.1 19.9 %copy-start.108 = (f32[1104]{0:T(1024)}, f32[1104]{0:T(1024)S(1)}, u32[]{:S(2)}) copy-start(f32[1104]{0:T(1024)S(1)} %broadcast_multiply_fusion.9) | copy-start | bytes 13252
  388.6 19.5 %copy-start.121 = (f32[1104]{0:T(1024)}, f32[1104]{0:T(1024)S(1)}, u32[]{:S(2)}) copy-start(f32[1104]{0:T(1024)S(1)} %add_rsqrt_fusion.1) | copy-start | bytes 13252
  388.6 15.2 %copy-start.140 = (f32[300]{0:T(512)}, f32[300]{0:T(512)S(1)}, u32[]{:S(2)}) copy-start(f32[300]{0:T(512)S(1)} %get-tuple-element.640) | copy-start | bytes 3604
  388.7 19.4 %copy-start.132 = (f32[300]{0:T(512)}, f32[300]{0:T(512)S(1)}, u32[]{:S(2)}) copy-start(f32[300]{0:T(512)S(1)} %get-tuple-element.643) | copy-start | bytes 3604
  394.5 9.4 copy-start.42
  394.6 9.3 copy-start.110
  395.0 8.9 copy-start.123
  465.1 196.4 %all-reduce.10.cloned.1.call-start = ((), (), s32[]{:S(2)}) async-start(), calls=%async_computation.2 | async-start | bytes 245760 | tf_op jit(solution)/shard_map/psum | solution.py:312
  485.8 8.7 copy-start.118
  490.3 9.2 copy-start.99
  490.3 9.2 copy-start.103
  490.3 9.3 copy-start.107
  495.9 6.8 copy-start.82
  499.6 8.3 slice-start
  537.0 7.0 copy-start.155
  537.0 7.0 copy-start.154
  537.0 7.0 copy-start.135
  537.0 7.0 copy-start.134
  569.0 375.9 %all-reduce.8.cloned.1.call-start = ((), (), s32[]{:S(2)}) async-start(), calls=%async_computation.1 | async-start | bytes 18739200
  580.1 6.5 copy-start.62
  649.2 12.4 %copy-start.91 = (f32[80,300]{1,0:T(8,128)S(1)}, f32[80,300]{1,0:T(8,128)}, u32[]{:S(2)}) copy-start(f32[80,300]{1,0:T(8,128)} %convolution_bitcast_fusion.2) | copy-start | bytes 288004
  649.2 13.7 %copy-start.46 = (bf16[1024,300]{0,1:T(8,128)(2,1)S(1)}, bf16[1024,300]{0,1:T(8,128)(2,1)}, u32[]{:S(2)}) copy-start(bf16[1024,300]{0,1:T(8,128)(2,1)} %get-tuple-element.719) | copy-start | bytes 1843204
  666.2 7.6 copy-start.44
  774.1 170.8 %copy-start.70 = (f32[2,36600]{1,0:T(2,128)S(1)}, f32[2,36600]{1,0:T(2,128)}, u32[]{:S(2)}) copy-start(f32[2,36600]{1,0:T(2,128)} %param.23) | copy-start | bytes 878404
  774.1 170.8 %copy-start.93 = (f32[2,36600]{1,0:T(2,128)S(1)}, f32[2,36600]{1,0:T(2,128)}, u32[]{:S(2)}) copy-start(f32[2,36600]{1,0:T(2,128)} %param.25) | copy-start | bytes 878404
  774.1 170.8 %copy-start.94 = (f32[2,36600]{1,0:T(2,128)S(1)}, f32[2,36600]{1,0:T(2,128)}, u32[]{:S(2)}) copy-start(f32[2,36600]{1,0:T(2,128)} %param.24) | copy-start | bytes 878404
  (120 other events, 454.0 us)
Sparse Core Ops, SparseCore 0:
  11.6 66.3 all-gather.12
  465.2 29.2 all-reduce.11
  569.1 31.4 all-reduce.9
  753.4 191.3 all-reduce.7
where the time goes:
time: 973 us; the launch traced here: 955 us
  local copies, waits for them, and re-layouts  445 us (46%)
  waiting for transfers between devices  213 us (22%)
  matrix products  198 us (20%)
  other arithmetic  49.8 us (5%)
  blocking collectives  32.5 us (3%)
  between operations  16.3 us (2%)
    unnamed x5, waiting for transfers between devices  163 us
    concatenate x2, local copies, waits for them, and re-layouts, backward_layer(): jnp.concatenate([w_query_grad.reshape(-1), w_key_grad.reshape(-1), w_valu...  87.4 us
    unnamed x338, local copies, waits for them, and re-layouts  63.7 us
    dot_general x22, matrix products, back_dot(): lax.dot_general(grad_in, matrix, (((1,), (1,)), ((), ())), preferred_elem...  53.5 us
    slice x1, local copies, waits for them, and re-layouts, local(): layer_params = [split_params(ordered[i], D, FF) for i in range(LAYERS)]  49 us
    dot_general x22, matrix products, contract(): lax.dot_general(left, right, (((0,), (0,)), ((), ())), preferred_element_...  48.5 us
    all_gather x1, waiting for transfers between devices, local(): lax.all_gather(weights.astype(jnp.bfloat16), ('graph', 'leaf'), axis=1, t...  47.8 us
    dot_general x22, matrix products, matmul(): return jnp.dot(left, right, preferred_element_type=jnp.float32)  47.3 us
  transfers between devices with their start and end apart: 4, of which 3 were waited for; matrix products, arithmetic and copies ran while one was open for 17% of the time, Pallas kernels for 0%

commit v1 on v0

v1 whole, which is shorter than its diff:
```python
import math

import jax
import jax.numpy as jnp
from jax import lax
from jax.experimental import pallas as pl
from jax.experimental.pallas import tpu as pltpu
from jax.sharding import PartitionSpec as P

D = 300
HEADS = 12
HEAD = 25
FF = 1200
LAYERS = 2
STEP = 5
ROWS_LAYER = 5 * D + 2 * FF + 4

NEG = -1e30
EPS_NORM = 1e-05
BETA_ONE = 0.9
BETA_TWO = 0.999
RATE = 0.05
DECAY = 0.01
EPS_ADAM = 1e-08
INV_ROOT_TWO = 0.7071067811865476
INV_ROOT_TWO_PI = 0.3989422804014327

HALO = 128
TILE = 256
HP = 16
PACK = 320
CHUNKS = tuple((i, min(i + 256, FF)) for i in range(0, FF, 256))
VMEM = 56 << 20
F32 = jnp.float32
BF = jnp.bfloat16

WEIGHTS = ("wq", "wk", "wv", "wo", "we", "w1", "w2", "norm")
WEIGHT_SHAPES = tuple([((D, D), BF)] * 5 + [((D, FF), BF), ((FF, D), BF), ((8, D), F32)])


def nn(a, b):
    return lax.dot_general(a, b, (((1,), (0,)), ((), ())), preferred_element_type=F32)


def nt(a, b):
    return lax.dot_general(a, b, (((1,), (1,)), ((), ())), preferred_element_type=F32)


def tn(a, b):
    return lax.dot_general(a, b, (((0,), (0,)), ((), ())), preferred_element_type=F32)


def halves(x):
    high = x.astype(BF)
    return high, (x - high.astype(F32)).astype(BF)


def thirds(x):
    high = x.astype(BF)
    rest = x - high.astype(F32)
    mid = rest.astype(BF)
    return high, mid, (rest - mid.astype(F32)).astype(BF)


def stacked(parts, axis=0):
    return jnp.concatenate([p.astype(F32) for p in parts], axis=axis).astype(BF)


def table(rows, repeat=1):
    head = lax.broadcasted_iota(jnp.int32, (repeat * rows, D), 0) % rows
    feature = lax.broadcasted_iota(jnp.int32, (repeat * rows, D), 1)
    low = head * HEAD
    return jnp.where((feature >= low) & (feature < low + HEAD), 1.0, 0.0).astype(BF)


def head_sum(values):
    high, low = halves(values)
    tab = table(HP)
    return nt(high, tab) + nt(low, tab)


def head_sum_t(values):
    high, low = halves(values)
    tab = table(HP)
    return nt(tab, high) + nt(tab, low)


def spread(values):
    high, low = halves(values)
    tab = table(HP)
    return nn(high, tab) + nn(low, tab)


def spread_t(values):
    return tn(stacked(halves(values)), table(HP, 2))


def onehot_col(ids, stars, repeat):
    lane = lax.broadcasted_iota(jnp.int32, (ids.shape[0], repeat * stars), 1)
    hit = lane == ids
    for i in range(1, repeat):
        hit = hit | (lane == ids + i * stars) & (ids >= 0)
    return jnp.where(hit, 1.0, 0.0).astype(BF)


def onehot_row(ids, stars, repeat):
    sub = lax.broadcasted_iota(jnp.int32, (repeat * stars, ids.shape[1]), 0)
    hit = sub == ids
    for i in range(1, repeat):
        hit = hit | (sub == ids + i * stars) & (ids >= 0)
    return jnp.where(hit, 1.0, 0.0).astype(BF)


def row_mean(x):
    return jnp.sum(x, axis=-1, keepdims=True) * (1.0 / D)


def normalized(x):
    dev = x - row_mean(x)
    inverse = lax.rsqrt(row_mean(dev * dev) + EPS_NORM)
    return dev * inverse, inverse


def norm_back(grad, scaled, inverse):
    return inverse * (grad - row_mean(grad) - scaled * row_mean(grad * scaled))


def ffn_forward(r, z, rows):
    norm = r["norm"]
    g1, b1, g2, b2 = (norm[i : i + 1, :] for i in range(4))
    xh1, inv1 = normalized(z)
    h = xh1 * g1 + b1
    hb = h.astype(BF)
    r["hb"][rows, :] = hb
    r["xh1"][rows, :] = xh1.astype(BF)
    r["inv1"][rows, :] = inv1
    total = h
    for lo, hi in CHUNKS:
        pre = nn(hb, r["w1"][:, lo:hi])
        cdf = 0.5 * (1.0 + lax.erf(pre * INV_ROOT_TWO))
        act = (pre * cdf).astype(BF)
        r["act"][rows, lo:hi] = act
        r["slope"][rows, lo:hi] = (
            cdf + pre * jnp.exp(-0.5 * pre * pre) * INV_ROOT_TWO_PI
        ).astype(BF)
        total = total + nn(act, r["w2"][lo:hi, :])
    xh2, inv2 = normalized(total)
    r["xh2"][rows, :] = xh2.astype(BF)
    r["inv2"][rows, :] = inv2
    return xh2 * g2 + b2


def fold(x):
    return jnp.sum(x.reshape(x.shape[0] // 8, 8, x.shape[1]), axis=0)


def ffn_backward(r, gy, rows, weight):
    norm = r["norm"]
    g1, g2 = norm[0:1, :], norm[2:3, :]
    xh2 = r["xh2"][rows, :].astype(F32)
    gw = gy * weight
    r["dn"][2] += fold(gw * xh2)
    r["dn"][3] += fold(gw)
    mid = norm_back(gy * g2, xh2, r["inv2"][rows, :])
    branch = mid.astype(BF)
    r["dbr"][rows, :] = (mid * weight).astype(BF)
    total = mid
    for lo, hi in CHUNKS:
        dact = nt(branch, r["w2"][lo:hi, :])
        dpre = dact * r["slope"][rows, lo:hi].astype(F32)
        low = dpre.astype(BF)
        r["dpre"][rows, lo:hi] = (dpre * weight).astype(BF)
        total = total + nt(low, r["w1"][:, lo:hi])
    xh1 = r["xh1"][rows, :].astype(F32)
    gw = total * weight
    r["dn"][0] += fold(gw * xh1)
    r["dn"][1] += fold(gw)
    return norm_back(total * g1, xh1, r["inv1"][rows, :])


def forward(r, stars, leaf_rows):
    centers = pl.ds(leaf_rows, stars)
    xc = r["xc"][...].astype(F32)
    low = xc.astype(BF)
    qs = nn(low, r["wq"][...]) * r["scale"][...]
    kc = nn(low, r["wk"][...])
    vc = nn(low, r["wv"][...])
    own_score = head_sum(qs * kc)
    r["qs"][...] = qs
    r["kc"][...] = kc
    r["vc"][...] = vc
    r["self"][...] = own_score
    r["qcat"][...] = stacked(halves(qs))
    r["xcat"][...] = stacked(halves(xc))

    def tile(t, carry):
        start = pl.multiple_of(t * TILE, TILE)
        rows = pl.ds(start, TILE)
        el = r["el"][rows, :]
        ew = el.astype(F32)
        xl = r["xl"][rows, :].astype(F32)
        r["en"][rows, :] = nn(el, r["we"][...]).astype(BF)
        hot = onehot_col(r["idc"][rows, :], stars, 2)
        m = (xl * ew).astype(BF)
        k = nn(m, r["wk"][...])
        r["k"][rows, :] = k.astype(BF)
        r["v"][rows, :] = nn(m, r["wv"][...]).astype(BF)
        r["s"][:, rows] = head_sum_t(nn(hot, r["qcat"][...]) * k)
        mc = (nn(hot, r["xcat"][...]) * ew).astype(BF)
        ub = nn(mc, r["wv"][...]).astype(BF)
        r["ub"][rows, :] = ub
        r["yl"][rows, :] = ffn_forward(r, xl + nn(ub, r["wo"][...]), rows)
        return carry

    lax.fori_loop(0, leaf_rows // TILE, tile, 0)

    ids = r["idr"][...]
    live = r["live"][...] > 0.5
    score = r["s"][...]
    top = jnp.where(live, score, NEG)
    lane = lax.broadcasted_iota(jnp.int32, (1, leaf_rows), 1)
    shift = 1
    while shift < 128:
        same = (pltpu.roll(ids, shift, 1) == ids) & (lane >= shift)
        top = jnp.maximum(top, jnp.where(same, pltpu.roll(top, shift, 1), NEG))
        shift *= 2
    hot_row = onehot_row(ids, stars, 1)
    last = hot_row.astype(F32) * r["last"][...]
    present = jnp.sum(last, axis=1, keepdims=True) > 0.5
    last = last.astype(BF)
    star_top = sum(nt(last, part) for part in thirds(top))
    peak = jnp.where(present, jnp.maximum(star_top, own_score), own_score)
    peak_row = tn(stacked(thirds(peak)), onehot_row(ids, stars, 3))
    e = jnp.where(live, jnp.exp(jnp.where(live, score - peak_row, 0.0)), 0.0)
    self_weight = jnp.exp(own_score - peak)
    total = self_weight + sum(nt(hot_row, part) for part in halves(e))
    r["logt"][...] = peak + jnp.log(total)
    weighted = (spread_t(e) * r["v"][...].astype(F32)).astype(BF)
    o = (nn(hot_row, weighted) + spread(self_weight) * vc) / spread(total)
    r["o"][...] = o
    z = xc + nn(o.astype(BF), r["wo"][...])
    r["yc"][...] = ffn_forward(r, z, centers)


def backward(r, stars, leaf_rows, own_rows):
    centers = pl.ds(leaf_rows, stars)
    own = r["cown"][...]
    r["dn"][...] = jnp.zeros_like(r["dn"])
    r["dq"][...] = jnp.zeros_like(r["dq"])
    r["dx"][...] = jnp.zeros_like(r["dx"])
    dz_c = ffn_backward(r, r["gyc"][...].astype(F32), centers, own)
    dac = dz_c.astype(BF)
    do = nt(dac, r["wo"][...])
    r["docat"][...] = stacked(halves(do))
    o = r["o"][...]
    vc = r["vc"][...]
    kc = r["kc"][...]
    qs = r["qs"][...]
    xc = r["xc"][...].astype(F32)
    r["qcat"][...] = stacked(halves(qs))
    r["xcat"][...] = stacked(halves(xc))
    delta = head_sum(do * o)
    self_p = jnp.exp(r["self"][...] - r["logt"][...])
    d_self = self_p * (head_sum(do * vc) - delta)
    coef_c = spread(d_self)
    dvc = spread(self_p) * do
    dkc = coef_c * qs
    logt_parts = stacked(thirds(r["logt"][...]))
    delta_parts = stacked(thirds(delta))

    def tile(t, carry):
        start = pl.multiple_of(t * TILE, TILE)
        rows = pl.ds(start, TILE)
        row = lax.broadcasted_iota(jnp.int32, (TILE, 1), 0) + start
        mine = jnp.where((row >= HALO) & (row < HALO + own_rows), 1.0, 0.0)
        dz = ffn_backward(r, r["gyl"][rows, :].astype(F32), rows, mine)
        dal = dz.astype(BF)
        r["dal"][rows, :] = dal
        du = nt(dal, r["wo"][...]).astype(BF)
        r["du"][rows, :] = du
        dmc = nt(du, r["wv"][...])
        el = r["el"][rows, :].astype(F32)
        xl = r["xl"][rows, :].astype(F32)
        hot = onehot_col(r["idc"][rows, :], stars, 2)
        ids_row = r["idr"][:, rows]
        hot_row = onehot_row(ids_row, stars, 1)
        hot3 = onehot_row(ids_row, stars, 3)
        xr = nn(hot, r["xcat"][...])
        r["mc"][rows, :] = (xr * el).astype(BF)
        r["dx"][...] += nn(hot_row, (dmc * el).astype(BF))
        de = dmc * xr
        live = r["live"][:, rows] > 0.5
        score = r["s"][:, rows] - tn(logt_parts, hot3)
        p = jnp.where(live, jnp.exp(jnp.where(live, score, 0.0)), 0.0)
        dor = nn(hot, r["docat"][...])
        v = r["v"][rows, :].astype(F32)
        ds = p * (head_sum_t(dor * v) - tn(delta_parts, hot3))
        dv = (spread_t(p) * dor).astype(BF)
        r["dv"][rows, :] = dv
        coef = spread_t(ds)
        r["dq"][...] += nn(hot_row, (coef * r["k"][rows, :].astype(F32)).astype(BF))
        dk = (coef * nn(hot, r["qcat"][...])).astype(BF)
        r["dk"][rows, :] = dk
        r["m"][rows, :] = (xl * el).astype(BF)
        dm = nt(dk, r["wk"][...]) + nt(dv, r["wv"][...])
        r["gxl"][rows, :] = dz + dm * el
        de = de + dm * xl + nt(r["ge"][rows, :], r["we"][...])
        r["gel"][rows, :] = de.astype(r["gel"].dtype)
        return carry

    lax.fori_loop(0, leaf_rows // TILE, tile, 0)

    dq = (r["dq"][...] + coef_c * kc) * r["scale"][...]
    dq_low = dq.astype(BF)
    dkc_low = dkc.astype(BF)
    dvc_low = dvc.astype(BF)
    r["gxc"][...] = (
        dz_c
        + nt(dq_low, r["wq"][...])
        + nt(dkc_low, r["wk"][...])
        + nt(dvc_low, r["wv"][...])
        + r["dx"][...]
    )

    own_leaf = slice(HALO, HALO + own_rows)
    nat = r["nat"]
    xb = xc.astype(BF)
    nat_store(nat, pl.ds(0, D), tn(xb, (dq * own).astype(BF)))
    m = r["m"][own_leaf, :]
    nat_store(
        nat, pl.ds(D, D), tn(m, r["dk"][own_leaf, :]) + tn(xb, (dkc * own).astype(BF))
    )
    nat_store(
        nat,
        pl.ds(2 * D, D),
        tn(m, r["dv"][own_leaf, :])
        + tn(r["mc"][own_leaf, :], r["du"][own_leaf, :])
        + tn(xb, (dvc * own).astype(BF)),
    )
    nat_store(
        nat,
        pl.ds(3 * D, D),
        tn(r["ub"][own_leaf, :], r["dal"][own_leaf, :]) + tn(o.astype(BF), (dz_c * own).astype(BF)),
    )
    nat_store(nat, pl.ds(4 * D, D), tn(r["el"][own_leaf, :], r["ge"][own_leaf, :]))
    base = 5 * D
    for j in range(FF // D):
        columns = slice(j * D, (j + 1) * D)
        part = tn(r["hb"][own_leaf, :], r["dpre"][own_leaf, columns]) + tn(
            r["hb"][leaf_rows:, :], r["dpre"][leaf_rows:, columns]
        )
        nat_store(nat, pl.ds(base + j, D, stride=FF // D), part)
    base = base + FF
    for lo, hi in CHUNKS:
        part = tn(r["act"][own_leaf, lo:hi], r["dbr"][own_leaf, :]) + tn(
            r["act"][leaf_rows:, lo:hi], r["dbr"][leaf_rows:, :]
        )
        nat_store(nat, pl.ds(base + lo, hi - lo), part)
    base = base + FF
    sums = [jnp.sum(r["dn"][i], axis=0, keepdims=True) for i in range(4)]
    nat_store(nat, pl.ds(base, 4), jnp.concatenate(sums, axis=0))


def nat_load(nat, at):
    return jnp.concatenate([nat[c, at, :] for c in range(3)], axis=1)[:, :D]


def nat_store(nat, at, value):
    nat[0, at, :] = value[:, 0:128]
    nat[1, at, :] = value[:, 128:256]
    rest = jnp.zeros((value.shape[0], 384 - D), F32)
    nat[2, at, :] = jnp.concatenate([value[:, 256:D], rest], axis=1)


def pack_blocks(r, holders, rows):
    nat = r["nat"]
    lane = lax.broadcasted_iota(jnp.int32, (64, 128), 1)
    for b in range(holders):
        at = r["slot"][b]
        top = b * rows
        r["out"][at, 0:128, :] = nat[0, top : top + 128, :].astype(BF)
        r["out"][at, 128:256, :] = nat[1, top : top + 128, :].astype(BF)
        high = pltpu.roll(nat[2, top + 64 : top + 128, :], 64, 1)
        tail = jnp.where(lane < 64, nat[2, top : top + 64, :], high)
        r["out"][at, 256:320, :] = tail.astype(BF)


def unpack_blocks(r, holders, rows):
    nat = r["nat"]
    for b in range(holders):
        at = r["slot"][b]
        top = b * rows
        nat[0, top : top + rows, :] = r["got"][at, 0:128, :].astype(F32)[:rows]
        nat[1, top : top + rows, :] = r["got"][at, 128:256, :].astype(F32)[:rows]
        tail = r["got"][at, 256:320, :].astype(F32)
        nat[2, top : top + 64, :] = tail
        nat[2, top + 64 : top + rows, :] = pltpu.roll(tail, 64, 1)[: rows - 64]
    for i, name in enumerate(WEIGHTS[:5]):
        r[name][...] = nat_load(nat, pl.ds(i * D, D)).astype(BF)
    base = 5 * D
    for j in range(FF // D):
        part = nat_load(nat, pl.ds(base + j, D, stride=FF // D))
        r["w1"][:, j * D : (j + 1) * D] = part.astype(BF)
    base = base + FF
    r["w2"][...] = nat_load(nat, pl.ds(base, FF)).astype(BF)
    base = base + FF
    r["norm"][...] = nat_load(nat, pl.ds(base, 8))


def call(body, inputs, outputs, scratch, in_smem=(), name=None):
    names = list(inputs) + list(outputs) + list(scratch)

    def kernel(*refs):
        body(dict(zip(names, refs, strict=True)))

    vmem = pl.BlockSpec(memory_space=pltpu.VMEM)
    smem = pl.BlockSpec(memory_space=pltpu.SMEM)
    results = pl.pallas_call(
        kernel,
        out_shape=[jax.ShapeDtypeStruct(s, d) for s, d in outputs.values()],
        in_specs=[smem if k in in_smem else vmem for k in inputs],
        out_specs=[vmem] * len(outputs),
        scratch_shapes=[pltpu.VMEM(s, d) for s, d in scratch.values()],
        compiler_params=pltpu.CompilerParams(vmem_limit_bytes=VMEM),
        name=name,
    )(*inputs.values())
    return dict(zip(outputs, results, strict=True))


def saved_shapes(stars, leaf_rows):
    rows = leaf_rows + stars
    return {
        "k": ((leaf_rows, D), BF),
        "v": ((leaf_rows, D), BF),
        "ub": ((leaf_rows, D), BF),
        "hb": ((rows, D), BF),
        "xh1": ((rows, D), BF),
        "xh2": ((rows, D), BF),
        "act": ((rows, FF), BF),
        "slope": ((rows, FF), BF),
        "inv1": ((rows, 1), F32),
        "inv2": ((rows, 1), F32),
        "s": ((HP, leaf_rows), F32),
        "qs": ((stars, D), F32),
        "kc": ((stars, D), F32),
        "vc": ((stars, D), F32),
        "o": ((stars, D), F32),
        "self": ((stars, HP), F32),
        "logt": ((stars, HP), F32),
    }


def forward_scratch(stars):
    return {"qcat": ((2 * stars, D), BF), "xcat": ((2 * stars, D), BF)}


def backward_scratch(stars, leaf_rows):
    rows = leaf_rows + stars
    return {
        "docat": ((2 * stars, D), BF),
        "dn": ((4, 8, D), F32),
        "dq": ((stars, D), F32),
        "dx": ((stars, D), F32),
        "dbr": ((rows, D), BF),
        "dpre": ((rows, FF), BF),
        "dal": ((leaf_rows, D), BF),
        "du": ((leaf_rows, D), BF),
        "mc": ((leaf_rows, D), BF),
        "dv": ((leaf_rows, D), BF),
        "dk": ((leaf_rows, D), BF),
        "m": ((leaf_rows, D), BF),
    }


def tree_stages(graph_size, leaf_size):
    stages = [("leaf", 0, 1)]
    for axis, size, first in (("leaf", leaf_size, 1), ("graph", graph_size, 0)):
        bit = first
        while (1 << bit) < size:
            bits = 1 if axis == "graph" and bit == 0 else min(2, size.bit_length() - 1 - bit)
            stages.append((axis, bit, bits))
            bit += bits
    return stages


def exchange(x, stage, value, sizes):
    axis, shift, bits = stage
    return lax.ppermute(x, axis, [(i, i ^ (value << shift)) for i in range(sizes[axis])])


def gather_tree(x, stages, sizes):
    held = x[None]
    for stage in stages[::-1]:
        held = jnp.concatenate(
            [held] + [exchange(held, stage, v, sizes) for v in range(1, 1 << stage[2])], axis=0
        )
    return held


def reduce_tree(x, stages, sizes):
    held = x
    for n, stage in enumerate(stages):
        count = held.shape[0] >> stage[2]
        total = held[:count].astype(F32)
        for v in range(1, 1 << stage[2]):
            total = total + exchange(held[v * count : (v + 1) * count], stage, v, sizes).astype(F32)
        held = total if n == len(stages) - 1 else total.astype(BF)
    return held[0]


def tree_slot(relative, stages, leaf_bits):
    slot = jnp.zeros_like(relative)
    for axis, shift, bits in stages:
        shift = shift + (leaf_bits if axis == "graph" else 0)
        slot = (slot << bits) | ((relative >> shift) & ((1 << bits) - 1))
    return slot


def to_rows(flat, rows):
    block = jnp.pad(flat.reshape(rows, D), ((0, 128 - rows), (0, 0)))
    tail = jnp.pad(block[:, 256:], ((0, 0), (0, 320 - D)))
    return jnp.concatenate(
        [block[:, :128], block[:, 128:256], jnp.concatenate([tail[:64], tail[64:]], axis=1)], axis=0
    )


def from_rows(packed, rows):
    tail = jnp.concatenate([packed[256:, : D - 256], packed[256:, 64 : D - 192]], axis=0)
    block = jnp.concatenate([packed[:128], packed[128:256], tail], axis=1)
    return block[:rows].reshape(-1)


def split_flat(vec):
    square = D * D
    mats = [vec[i * square : (i + 1) * square].reshape(D, D) for i in range(5)]
    at = 5 * square
    w1 = vec[at : at + D * FF].reshape(D, FF)
    at = at + D * FF
    w2 = vec[at : at + FF * D].reshape(FF, D)
    at = at + FF * D
    norm = jnp.pad(vec[at : at + 4 * D].reshape(4, D).astype(F32), ((0, 4), (0, 0)))
    return dict(zip(WEIGHTS, mats + [w1, w2, norm], strict=True))


def with_halo(x):
    size = lax.axis_size("leaf")
    left = lax.ppermute(x[:, -HALO:], "leaf", [(i, i + 1) for i in range(size - 1)])
    right = lax.ppermute(x[:, :HALO], "leaf", [(i + 1, i) for i in range(size - 1)])
    return jnp.concatenate([left, x, right], axis=1)


def local(
    weights,
    first_moment,
    second_moment,
    centers,
    leaves,
    edge_feats,
    center_cot,
    leaf_cot,
    edge_cot,
    graph_ids,
    star_sizes,
    leaf_mask,
    owner_list,
):
    sizes = {"graph": lax.axis_size("graph"), "leaf": lax.axis_size("leaf")}
    holders = sizes["graph"] * sizes["leaf"]
    block_len = weights.shape[1]
    block_rows = block_len // D
    in_rows = block_len % D == 0 and 64 < block_rows <= 128
    stars = centers.shape[1]
    own_rows = leaves.shape[1]
    leaf_rows = own_rows + 2 * HALO

    stages = tree_stages(sizes["graph"], sizes["leaf"])
    me = lax.axis_index(("graph", "leaf"))
    slot = tree_slot(owner_list ^ me, stages, sizes["leaf"].bit_length() - 1)
    nat_rows = ROWS_LAYER + 12
    weights_low = weights.astype(BF)
    params = []
    for i in range(LAYERS):
        if in_rows:
            got = gather_tree(to_rows(weights_low[i], block_rows), stages, sizes)
            params.append(
                call(
                    lambda r: unpack_blocks(r, holders, block_rows),
                    {"slot": slot, "got": got},
                    dict(zip(WEIGHTS, WEIGHT_SHAPES, strict=True)),
                    {"nat": ((3, nat_rows, 128), F32)},
                    in_smem=("slot",),
                    name="unpack",
                )
            )
        else:
            got = gather_tree(weights_low[i], stages, sizes)
            params.append(split_flat(jnp.take(got, slot, axis=0).reshape(-1)))

    ext = with_halo(jnp.concatenate([leaves, edge_feats, leaf_cot, edge_cot], axis=0))
    code = with_halo(graph_ids * 2 + leaf_mask + 1) - 1
    ids = jnp.where(code < 0, -1, code >> 1)
    live = jnp.where(code < 0, 0, code & 1).astype(F32)
    edge_id = jnp.full((1, 1), -1, jnp.int32)
    last = (ids != jnp.concatenate([ids[:, 1:], edge_id], axis=1)).astype(F32)
    first = graph_ids[0] != ids[0, HALO - 1 : HALO - 1 + own_rows]
    star_index = jnp.arange(stars, dtype=jnp.int32)
    star_own = jnp.any((star_index[:, None] == graph_ids) & first[None, :], axis=1)[:, None]
    scale = (jnp.log(star_sizes[0].astype(F32)) / (math.log(32.0) * math.sqrt(HEAD)))[:, None]
    base = {
        "idc": ids.reshape(-1, 1),
        "idr": ids,
        "live": live,
        "last": last,
        "scale": scale,
        "cown": star_own.astype(F32),
    }
    saved = saved_shapes(stars, leaf_rows)
    f_scratch = forward_scratch(stars)
    b_scratch = backward_scratch(stars, leaf_rows)
    nat = {"nat": ((3, nat_rows, 128), F32)}
    blocks = {"out": ((holders, PACK, 128), BF)}
    grads_out = blocks if in_rows else nat
    grads_scratch = nat if in_rows else {}

    one = call(
        lambda r: forward(r, stars, leaf_rows),
        {**base, **params[0], "xc": centers[0], "xl": ext[0], "el": ext[1]},
        {
            "yc": ((stars, D), F32),
            "yl": ((leaf_rows, D), F32),
            "en": ((leaf_rows, D), BF),
            **saved,
        },
        f_scratch,
        name="forward",
    )

    def both(r):
        forward(r, stars, leaf_rows)
        backward(r, stars, leaf_rows, own_rows)
        if in_rows:
            pack_blocks(r, holders, block_rows)

    two = call(
        both,
        {
            **base,
            "slot": slot,
            **params[1],
            "xc": one["yc"],
            "xl": one["yl"],
            "el": one["en"],
            "gyc": center_cot[0],
            "gyl": ext[2],
            "ge": ext[3],
        },
        {
            "yc": ((stars, D), F32),
            "yl": ((leaf_rows, D), F32),
            "en": ((leaf_rows, D), BF),
            "gxc": ((stars, D), F32),
            "gxl": ((leaf_rows, D), F32),
            "gel": ((leaf_rows, D), BF),
            **grads_out,
        },
        {**f_scratch, **saved, **b_scratch, **grads_scratch},
        in_smem=("slot",),
        name="last",
    )

    def back(r):
        backward(r, stars, leaf_rows, own_rows)
        if in_rows:
            pack_blocks(r, holders, block_rows)

    three = call(
        back,
        {
            **base,
            "slot": slot,
            **params[0],
            "xc": centers[0],
            "xl": ext[0],
            "el": ext[1],
            "gyc": two["gxc"],
            "gyl": two["gxl"],
            "ge": two["gel"],
            **{k: one[k] for k in saved},
        },
        {
            "gxc": ((stars, D), F32),
            "gxl": ((leaf_rows, D), F32),
            "gel": ((leaf_rows, D), F32),
            **grads_out,
        },
        {**f_scratch, **b_scratch, **grads_scratch},
        in_smem=("slot",),
        name="first",
    )

    totals = []
    for grads in (three, two):
        if in_rows:
            totals.append(from_rows(reduce_tree(grads["out"], stages, sizes), block_rows))
        else:
            flat = jnp.swapaxes(grads["nat"][:, :ROWS_LAYER], 0, 1).reshape(ROWS_LAYER, 384)
            flat = flat[:, :D].reshape(holders, block_len)
            placed = jnp.zeros_like(flat).at[slot].set(flat).astype(BF)
            totals.append(reduce_tree(placed, stages, sizes))
    grad_total = jnp.stack(totals)

    own_leaf = slice(HALO, HALO + own_rows)
    centers_out = lax.psum(jnp.where(star_own, two["yc"], 0.0).astype(BF), "leaf")
    grad_centers = lax.psum(jnp.where(star_own, three["gxc"], 0.0), "leaf")
    first_new = BETA_ONE * first_moment + (1.0 - BETA_ONE) * grad_total
    second_new = BETA_TWO * second_moment + (1.0 - BETA_TWO) * grad_total * grad_total
    step_one = first_new / (1.0 - BETA_ONE**STEP)
    step_two = second_new / (1.0 - BETA_TWO**STEP)
    weights_new = weights - RATE * (step_one / (jnp.sqrt(step_two) + EPS_ADAM) + DECAY * weights)
    return (
        centers_out[None],
        two["yl"][own_leaf].astype(BF)[None],
        two["en"][own_leaf][None],
        grad_centers[None],
        three["gxl"][own_leaf][None],
        three["gel"][own_leaf][None],
        first_new,
        second_new,
        weights_new,
        weights_new.astype(BF),
        grad_total,
    )


def solution(mesh):
    both = ("graph", "leaf")
    return jax.shard_map(
        local,
        mesh=mesh,
        in_specs=(
            P(None, both),
            P(None, both),
            P(None, both),
            P("graph", None, None),
            P("graph", "leaf", None),
            P("graph", "leaf", None),
            P("graph", None, None),
            P("graph", "leaf", None),
            P("graph", "leaf", None),
            P("graph", "leaf"),
            P("graph", None),
            P("graph", "leaf"),
            P(),
        ),
        out_specs=(
            P("graph", None, None),
            P("graph", "leaf", None),
            P("graph", "leaf", None),
            P("graph", None, None),
            P("graph", "leaf", None),
            P("graph", "leaf", None),
            P(None, both),
            P(None, both),
            P(None, both),
            P(None, both),
            P(None, both),
        ),
        check_vma=False,
    )
```

time: 973 us -> 315 us (0.32); the launches traced: 955 us -> 309 us
  local copies, waits for them, and re-layouts: 445 us -> 51 us
  matrix products: 198 us -> 0 us
  waiting for transfers between devices: 213 us -> 52.5 us
  Pallas kernels: 0 us -> 113 us
  starting transfers between devices: 0.16 us -> 38.6 us
  other arithmetic: 49.8 us -> 28.1 us
  blocking collectives: 32.5 us -> 11.9 us
    dot_general x112 -> x0, matrix products: 198 us -> none  [the longest x22 53.5 us: back_dot(): lax.dot_general(grad_in, matrix, (((1,), (1,)), ((), ())), preferred_elem...]
    unnamed x5 -> x1, waiting for transfers between devices: 163 us -> 0.02 us
    pallas_call x0 -> x5, Pallas kernels: none -> 113 us  [call(): pl.pallas_call(kernel, out_shape=[jax.ShapeDtypeStruct(s, d) for s, d in...]
    gather x24 -> x0, local copies, waits for them, and re-layouts: 88.5 us -> none  [the longest x4 15.6 us: backward_layer(): grad_att_rows = jnp.take(grad_attended, star_ids, axis=0)]
    concatenate x3 -> x4, local copies, waits for them, and re-layouts: 88 us -> 7.21 us  [gather_tree(): jnp.concatenate([held] + [exchange(held, stage, v, sizes) for v in range(...]
    reshape x20 -> x0, local copies, waits for them, and re-layouts: 70.5 us -> none  [the longest x2 21.1 us: local(): gathered.reshape(LAYERS, holders, block_len)]
    slice x8 -> x21, local copies, waits for them, and re-layouts: 78.6 us -> 8.63 us  [the longest x8 6.95 us: reduce_tree(): held[v * count:(v + 1) * count]]
    ppermute x0 -> x28, waiting for transfers between devices: none -> 52.4 us  [the longest x24 52.4 us: exchange(): lax.ppermute(x, axis, [(i, i ^ value << shift) for i in range(sizes[axis])])]
  transfers between devices with their start and end apart: 4 -> 29, of which waited for: 3 -> 8; matrix products, arithmetic and copies ran while one was open for 17% -> 23% of each run, Pallas kernels for 0% -> 12%
where the time goes in v1:
time: 315 us; the launch traced here: 309 us
  Pallas kernels  113 us (36%)
  waiting for transfers between devices  52.5 us (17%)
  local copies, waits for them, and re-layouts  51 us (16%)
  starting transfers between devices  38.6 us (12%)
  other arithmetic  28.1 us (9%)
  between operations  14.8 us (5%)
  blocking collectives  11.9 us (4%)
    pallas_call x5, Pallas kernels, call(): pl.pallas_call(kernel, out_shape=[jax.ShapeDtypeStruct(s, d) for s, d in...  113 us
    ppermute x24, waiting for transfers between devices, exchange(): lax.ppermute(x, axis, [(i, i ^ value << shift) for i in range(sizes[axis])])  52.4 us
    ppermute x24, starting transfers between devices, exchange(): lax.ppermute(x, axis, [(i, i ^ value << shift) for i in range(sizes[axis])])  29.7 us
    unnamed x63, local copies, waits for them, and re-layouts  24.9 us
    psum x1, blocking collectives, local(): lax.psum(jnp.where(star_own, two['yc'], 0.0).astype(BF), 'leaf')  11.9 us
    concatenate x4, local copies, waits for them, and re-layouts, gather_tree(): jnp.concatenate([held] + [exchange(held, stage, v, sizes) for v in range(...  7.21 us
    slice x8, local copies, waits for them, and re-layouts, reduce_tree(): held[v * count:(v + 1) * count]  6.95 us
  transfers between devices with their start and end apart: 29, of which 8 were waited for; matrix products, arithmetic and copies ran while one was open for 23% of the time, Pallas kernels for 12%

profile of v1, /device:TPU:0, one launch (start us, length us, event | category | flops | bytes accessed | tf_op | source)
XLA Modules:
  0.0 309.4 jit_solution(8563789389331128250)
XLA Ops:
  10.2 5.0 %collective-permute-start.4 = (bf16[1,320,128]{2,1,0:T(8,128)(2,1)S(1)}, bf16[1,320,128]{2,1,0:T(8,128)(2,1)S(1)}, u32[]{:S(2)}, u32[]{:S(2)}) collective-permute-start(bf16[1,320,128]{2,1,0:T(8,128)(2,1)S(1)} %get-tuple-element.170), channel_id=1, source_target_pairs={{0,24},{4,28},{8,16},{12,20},{16,8},{20,12},{24,0},{28,4},{1,25},{... | collective-permute-start | bytes 245768 | tf_op jit(solution)/shard_map/ppermute | solution.py:488
  16.6 1.3 collective-permute-start
  17.9 1.3 collective-permute-start.1
  21.9 1.4 copy.107
  27.0 3.8 %collective-permute-start.10 = (bf16[1,320,128]{2,1,0:T(8,128)(2,1)S(1)}, bf16[1,320,128]{2,1,0:T(8,128)(2,1)}, u32[]{:S(2)}, u32[]{:S(2)}) collective-permute-start(bf16[1,320,128]{2,1,0:T(8,128)(2,1)S(1)} %get-tuple-element.168), channel_id=1, source_target_pairs={{0,24},{4,28},{8,16},{12,20},{16,8},{20,12},{24,0},{28,4},{1,25},{... | collective-permute-start | bytes 245768 | tf_op jit(solution)/shard_map/ppermute | solution.py:488
  35.1 1.8 copy.103
  36.9 2.0 broadcast_select_fusion.refs_0_
  40.4 4.9 %collective-permute-start.14 = (bf16[4,128,300]{2,1,0:T(8,128)(2,1)}, bf16[4,128,300]{2,1,0:T(8,128)(2,1)}, u32[]{:S(2)}, u32[]{:S(2)}) collective-permute-start(bf16[4,128,300]{2,1,0:T(8,128)(2,1)} %get-tuple-element.179), channel_id=1, source_target_pairs={{0,1},{1,2},{2,3},{4,5},{5,6},{6,7},{8,9},{9,10},{10,11},{12,13},{... | collective-permute-start | bytes 921608 | tf_op jit(solution)/shard_map/ppermute | solution.py:547
  47.7 1.6 collective-permute-start.5
  51.5 1.6 constant_dynamic-update-slice_fusion.26
  53.1 1.6 constant_dynamic-update-slice_fusion.25
  54.7 1.6 constant_dynamic-update-slice_fusion.9
  56.3 1.6 constant_dynamic-update-slice_fusion.8
  58.7 5.2 %collective-permute-done.11 = bf16[4,320,128]{2,1,0:T(8,128)(2,1)S(1)} collective-permute-done((bf16[4,320,128]{2,1,0:T(8,128)(2,1)S(1)}, bf16[4,320,128]{2,1,0:T(8,128)(2,1)S(1)}, u32[]{:S(2)}, u32[]{:S(2)}) %collective-permute-start.11) | collective-permute-done | bytes 327712 | tf_op jit(solution)/shard_map/ppermute | solution.py:488
  65.0 4.0 %collective-permute-start.12 = (bf16[8,320,128]{2,1,0:T(8,128)(2,1)}, bf16[8,320,128]{2,1,0:T(8,128)(2,1)}, u32[]{:S(2)}, u32[]{:S(2)}) collective-permute-start(bf16[8,320,128]{2,1,0:T(8,128)(2,1)} %get-tuple-element.193), channel_id=1, source_target_pairs={{0,2},{1,3},{2,0},{3,1},{4,6},{5,7},{6,4},{7,5},{8,10},{9,11},{10,... | collective-permute-start | bytes 1966088 | tf_op jit(solution)/shard_map/ppermute | solution.py:488
  71.5 13.5 %collective-permute-done.12 = bf16[8,320,128]{2,1,0:T(8,128)(2,1)} collective-permute-done((bf16[8,320,128]{2,1,0:T(8,128)(2,1)}, bf16[8,320,128]{2,1,0:T(8,128)(2,1)}, u32[]{:S(2)}, u32[]{:S(2)}) %collective-permute-start.12) | collective-permute-done | bytes 655392 | tf_op jit(solution)/shard_map/ppermute | solution.py:488
  85.0 2.5 constant_dynamic-update-slice_fusion.23
  87.4 9.9 %collective-permute-done.6 = bf16[8,320,128]{2,1,0:T(8,128)(2,1)} collective-permute-done((bf16[8,320,128]{2,1,0:T(8,128)(2,1)}, bf16[8,320,128]{2,1,0:T(8,128)(2,1)}, u32[]{:S(2)}, u32[]{:S(2)}) %collective-permute-start.6) | collective-permute-done | bytes 655392 | tf_op jit(solution)/shard_map/ppermute | solution.py:488
  97.3 2.4 constant_dynamic-update-slice_fusion.5
  99.7 3.7 %pad_maximum_fusion = bf16[4,1280,300]{2,1,0:T(8,128)(2,1)S(1)} fusion(bf16[4,128,300]{2,1,0:T(8,128)(2,1)} %collective-permute-done.15, bf16[1,1024,300]{2,1,0:T(8,128)(2,1)S(1)} %copy.107, bf16[1,1024,300]{2,1,0:T(8,128)(2,1)S(1)} %copy.106, bf16[1,1024,300]{2,1,0:T(8,128)(2,1)S(1)} %copy.105, bf16[1,1024,300]{2,1,0:T(8,128)(2,1)S(1)} %copy.104, ...), kind=kLoop, calls=%fused_computation | loop fusion | flops 18432000 | bytes 6144000 | tf_op jit(solution)/shard_map/concatenate | solution.py:549
  103.4 2.0 slice_bitcast_fusion.2
  106.6 4.3 %unpack.3 = (bf16[300,300]{1,0:T(8,128)(2,1)}, bf16[300,300]{1,0:T(8,128)(2,1)}, bf16[300,300]{1,0:T(8,128)(2,1)}, bf16[300,300]{1,0:T(8,128)(2,1)}, bf16[300,30...) custom-call(s32[32]{0:T(128)} %and_or_fusion.refs_0_.refs_6_, ...), custom_call_target="tpu_custom_call" | custom-call | tf_op jit(solution)/shard_map/unpack/pallas_call | solution.py:418
  112.1 4.3 %unpack.2 = (bf16[300,300]{1,0:T(8,128)(2,1)}, bf16[300,300]{1,0:T(8,128)(2,1)}, bf16[300,300]{1,0:T(8,128)(2,1)}, bf16[300,300]{1,0:T(8,128)(2,1)}, bf16[300,30...) custom-call(s32[32]{0:T(128)} %and_or_fusion.refs_0_.refs_6_, ...), custom_call_target="tpu_custom_call" | custom-call | tf_op jit(solution)/shard_map/unpack/pallas_call | solution.py:418
  116.3 23.6 %forward.1 = (f32[80,300]{1,0:T(8,128)}, f32[1280,300]{1,0:T(8,128)}, bf16[1280,300]{1,0:T(8,128)(2,1)}, bf16[1280,300]{1,0:T(8,128)(2,1)}, bf16[1280,300]{1,0:T...) custom-call(s32[1280,1]{1,0:T(8,128)} %broadcast_select_fusion.refs_, ...), custom_call_target="tpu_custom_call" | custom-call | tf_op jit(solution)/shard_map/forward/pallas_call | solution.py:418
  140.0 46.6 %last.1 = (f32[80,300]{1,0:T(8,128)}, f32[1280,300]{1,0:T(8,128)}, bf16[1280,300]{1,0:T(8,128)(2,1)}, f32[80,300]{1,0:T(8,128)}, f32[1280,300]{1,0:T(8,128)}, /*...) custom-call(s32[1280,1]{1,0:T(8,128)} %broadcast_select_fusion.refs_0_, s32[1,1280]{1,0:T(1,128)} %copy-done.15, ...), custom_call_target="tpu_custom_call" | custom-call | tf_op jit(solution)/shard_map/last/pallas_call | solution.py:418
  186.6 2.5 slice.227
  189.6 33.7 %first.1 = (f32[80,300]{1,0:T(8,128)}, f32[1280,300]{1,0:T(8,128)}, f32[1280,300]{1,0:T(8,128)}, bf16[32,320,128]{2,1,0:T(8,128)(2,1)}) custom-call(s32[1280,1]{1,0:T(8,128)} %broadcast_select_fusion.refs_0_, s32[1,1280]{1,0:T(1,128)} %copy-done.15, f32[1,1280]{1,0:T(1,128)} %get-tuple-element.171.refs_2_, f32[1,1280]{1,0:T(1,128)} %compare_convert_fusion.refs_3_, ...), custom_call_target="tpu_custom_call" | custom-call | tf_op jit(solution)/shard_map/first/pallas_call | solution.py:418
  223.3 2.7 slice.210
  226.0 1.6 select_bitcast_fusion
  228.4 1.8 add_convert_fusion
  230.2 1.4 collective-permute-start.23
  231.6 1.7 add_convert_fusion.1
  235.5 13.3 %collective-permute-done.23 = bf16[8,320,128]{2,1,0:T(8,128)(2,1)S(1)} collective-permute-done((bf16[8,320,128]{2,1,0:T(8,128)(2,1)S(1)}, bf16[8,320,128]{2,1,0:T(8,128)(2,1)S(1)}, u32[]{:S(2)}, u32[]{:S(2)}) %collective-permute-start.23) | collective-permute-done | bytes 655392 | tf_op jit(solution)/shard_map/ppermute | solution.py:488
  250.7 1.5 collective-permute-start.24
  252.2 2.8 fusion
  255.0 2.2 copy.114
  257.2 2.2 copy.115
  259.4 2.0 copy.117
  261.4 2.0 copy.116
  263.4 11.9 %psum.14 = bf16[1,80,300]{2,1,0:T(8,128)(2,1)} all-reduce(bf16[1,80,300]{2,1,0:T(8,128)(2,1)} %fusion.6), channel_id=1, replica_groups=mesh['graph'=8,'leaf'=4] {'leaf'}, use_global_device_ids=true, to_apply=%region_1.2 | all-reduce | flops 24000 | bytes 96000 | tf_op jit(solution)/shard_map/psum | solution.py:713
  278.4 1.5 collective-permute-start.25
  279.9 2.4 collective-permute-start.27
  282.5 3.9 %collective-permute-done.18 = bf16[4,320,128]{2,1,0:T(8,128)(2,1)S(1)} collective-permute-done((bf16[4,320,128]{2,1,0:T(8,128)(2,1)S(1)}, bf16[4,320,128]{2,1,0:T(8,128)(2,1)S(1)}, u32[]{:S(2)}, u32[]{:S(2)}) %collective-permute-start.18) | collective-permute-done | bytes 327712 | tf_op jit(solution)/shard_map/ppermute | solution.py:488
  287.7 2.7 collective-permute-start.21
  292.3 2.6 collective-permute-done.21
  294.9 3.0 collective-permute-done.20
  298.4 2.4 fusion.8
  300.8 1.6 copy.149
  (148 shorter events, 39.7 us)
Async XLA Ops:
  7.2 13.6 %copy-start.10 = (bf16[1,1024,300]{1,2,0:T(8,128)(2,1)S(1)}, bf16[1,1024,300]{1,2,0:T(8,128)(2,1)}, u32[]{:S(2)}) copy-start(bf16[1,1024,300]{1,2,0:T(8,128)(2,1)} %param.17) | copy-start | bytes 1843204
  7.2 14.0 %copy-start.11 = (bf16[1,1024,300]{1,2,0:T(8,128)(2,1)S(1)}, bf16[1,1024,300]{1,2,0:T(8,128)(2,1)}, u32[]{:S(2)}) copy-start(bf16[1,1024,300]{1,2,0:T(8,128)(2,1)} %param.18) | copy-start | bytes 1843204
  7.2 14.3 %copy-start.12 = (bf16[1,1024,300]{1,2,0:T(8,128)(2,1)S(1)}, bf16[1,1024,300]{1,2,0:T(8,128)(2,1)}, u32[]{:S(2)}) copy-start(bf16[1,1024,300]{1,2,0:T(8,128)(2,1)} %param.20) | copy-start | bytes 1843204
  7.2 293.6 %all-reduce.6.cloned.1.call-start = ((), (), s32[]{:S(2)}) async-start(), calls=%async_computation | async-start | bytes 245760 | tf_op jit(solution)/shard_map/psum | solution.py:714
  10.2 29.5 %collective-permute-start.4 = (bf16[1,320,128]{2,1,0:T(8,128)(2,1)S(1)}, bf16[1,320,128]{2,1,0:T(8,128)(2,1)S(1)}, u32[]{:S(2)}, u32[]{:S(2)}) collective-permute-start(bf16[1,320,128]{2,1,0:T(8,128)(2,1)S(1)} %get-tuple-element.170), channel_id=1, source_target_pairs={{0,24},{4,28},{8,16},{12,20},{16,8},{20,12},{24,0},{28,4},{1,25},{... | collective-permute-start | bytes 245768 | tf_op jit(solution)/shard_map/ppermute | solution.py:488
  15.3 25.2 %collective-permute-start.3 = (bf16[1,320,128]{2,1,0:T(8,128)(2,1)S(1)}, bf16[1,320,128]{2,1,0:T(8,128)(2,1)}, u32[]{:S(2)}, u32[]{:S(2)}) collective-permute-start(bf16[1,320,128]{2,1,0:T(8,128)(2,1)S(1)} %get-tuple-element.170), channel_id=1, source_target_pairs={{0,16},{4,20},{8,24},{12,28},{16,0},{20,4},{24,8},{28,12},{1,17},{... | collective-permute-start | bytes 245768 | tf_op jit(solution)/shard_map/ppermute | solution.py:488
  15.3 30.1 %collective-permute-start.2 = (bf16[1,320,128]{2,1,0:T(8,128)(2,1)S(1)}, bf16[1,320,128]{2,1,0:T(8,128)(2,1)}, u32[]{:S(2)}, u32[]{:S(2)}) collective-permute-start(bf16[1,320,128]{2,1,0:T(8,128)(2,1)S(1)} %get-tuple-element.170), channel_id=1, source_target_pairs={{0,8},{4,12},{8,0},{12,4},{16,24},{20,28},{24,16},{28,20},{1,9},{5... | collective-permute-start | bytes 245768 | tf_op jit(solution)/shard_map/ppermute | solution.py:488
  16.6 10.5 %collective-permute-start = (s32[1,128]{1,0:T(1,128)S(1)}, s32[1,128]{1,0:T(1,128)S(1)}, u32[]{:S(2)}, u32[]{:S(2)}) collective-permute-start(s32[1,128]{1,0:T(1,128)S(1)} %get-tuple-element.235), channel_id=1, source_target_pairs={{0,1},{1,2},{2,3},{4,5},{5,6},{6,7},{8,9},{9,10},{10,11},{12,13},{... | collective-permute-start | bytes 1544 | tf_op jit(solution)/shard_map/ppermute | solution.py:547
  17.9 13.0 %collective-permute-start.1 = (s32[1,128]{1,0:T(1,128)S(1)}, s32[1,128]{1,0:T(1,128)S(1)}, u32[]{:S(2)}, u32[]{:S(2)}) collective-permute-start(s32[1,128]{1,0:T(1,128)S(1)} %get-tuple-element.236), channel_id=1, source_target_pairs={{1,0},{2,1},{3,2},{5,4},{6,5},{7,6},{9,8},{10,9},{11,10},{13,12},{... | collective-permute-start | bytes 1544 | tf_op jit(solution)/shard_map/ppermute | solution.py:548
  20.8 2.6 copy-start.21
  21.9 9.6 %copy-start.19 = (s32[1,1024]{1,0:T(1,128)S(1)}, s32[1,1024]{1,0:T(1,128)}, u32[]{:S(2)}) copy-start(s32[1,1024]{1,0:T(1,128)} %param.22) | copy-start | bytes 12292
  27.0 20.6 %collective-permute-start.10 = (bf16[1,320,128]{2,1,0:T(8,128)(2,1)S(1)}, bf16[1,320,128]{2,1,0:T(8,128)(2,1)}, u32[]{:S(2)}, u32[]{:S(2)}) collective-permute-start(bf16[1,320,128]{2,1,0:T(8,128)(2,1)S(1)} %get-tuple-element.168), channel_id=1, source_target_pairs={{0,24},{4,28},{8,16},{12,20},{16,8},{20,12},{24,0},{28,4},{1,25},{... | collective-permute-start | bytes 245768 | tf_op jit(solution)/shard_map/ppermute | solution.py:488
  30.9 18.4 %collective-permute-start.9 = (bf16[1,320,128]{2,1,0:T(8,128)(2,1)S(1)}, bf16[1,320,128]{2,1,0:T(8,128)(2,1)}, u32[]{:S(2)}, u32[]{:S(2)}) collective-permute-start(bf16[1,320,128]{2,1,0:T(8,128)(2,1)S(1)} %get-tuple-element.168), channel_id=1, source_target_pairs={{0,16},{4,20},{8,24},{12,28},{16,0},{20,4},{24,8},{28,12},{1,17},{... | collective-permute-start | bytes 245768 | tf_op jit(solution)/shard_map/ppermute | solution.py:488
  39.7 9.5 %collective-permute-start.8 = (bf16[1,320,128]{2,1,0:T(8,128)(2,1)S(1)}, bf16[1,320,128]{2,1,0:T(8,128)(2,1)S(1)}, u32[]{:S(2)}, u32[]{:S(2)}) collective-permute-start(bf16[1,320,128]{2,1,0:T(8,128)(2,1)S(1)} %get-tuple-element.168), channel_id=1, source_target_pairs={{0,8},{4,12},{8,0},{12,4},{16,24},{20,28},{24,16},{28,20},{1,9},{5... | collective-permute-start | bytes 245768 | tf_op jit(solution)/shard_map/ppermute | solution.py:488
  40.4 59.3 %collective-permute-start.14 = (bf16[4,128,300]{2,1,0:T(8,128)(2,1)}, bf16[4,128,300]{2,1,0:T(8,128)(2,1)}, u32[]{:S(2)}, u32[]{:S(2)}) collective-permute-start(bf16[4,128,300]{2,1,0:T(8,128)(2,1)} %get-tuple-element.179), channel_id=1, source_target_pairs={{0,1},{1,2},{2,3},{4,5},{5,6},{6,7},{8,9},{9,10},{10,11},{12,13},{... | collective-permute-start | bytes 921608 | tf_op jit(solution)/shard_map/ppermute | solution.py:547
  45.4 54.3 %collective-permute-start.15 = (bf16[4,128,300]{2,1,0:T(8,128)(2,1)}, bf16[4,128,300]{2,1,0:T(8,128)(2,1)}, u32[]{:S(2)}, u32[]{:S(2)}) collective-permute-start(bf16[4,128,300]{2,1,0:T(8,128)(2,1)} %get-tuple-element.180), channel_id=1, source_target_pairs={{1,0},{2,1},{3,2},{5,4},{6,5},{7,6},{9,8},{10,9},{11,10},{13,12},{... | collective-permute-start | bytes 921608 | tf_op jit(solution)/shard_map/ppermute | solution.py:548
  47.6 22.5 %copy-start.18 = (s32[1,1280]{1,0:T(1,128)S(1)}, s32[1,1280]{1,0:T(1,128)}, u32[]{:S(2)}) copy-start(s32[1,1280]{1,0:T(1,128)} %copy-done.17) | copy-start | bytes 15364
  47.6 22.5 %copy-start.20 = (s32[1,1279]{1,0:T(1,128)S(1)}, s32[1,1279]{1,0:T(1,128)}, u32[]{:S(2)}) copy-start(s32[1,1279]{1,0:T(1,128)} %slice.246) | copy-start | bytes 15352
  47.7 21.3 %collective-permute-start.5 = (bf16[4,320,128]{2,1,0:T(8,128)(2,1)S(1)}, bf16[4,320,128]{2,1,0:T(8,128)(2,1)S(1)}, u32[]{:S(2)}, u32[]{:S(2)}) collective-permute-start(bf16[4,320,128]{2,1,0:T(8,128)(2,1)S(1)} %pad_maximum_fusion.5), channel_id=1, source_target_pairs={{0,4},{4,0},{8,12},{12,8},{16,20},{20,16},{24,28},{28,24},{1,5},{5... | collective-permute-start | bytes 983048 | tf_op jit(solution)/shard_map/ppermute | solution.py:488
  50.2 13.7 %collective-permute-start.11 = (bf16[4,320,128]{2,1,0:T(8,128)(2,1)S(1)}, bf16[4,320,128]{2,1,0:T(8,128)(2,1)S(1)}, u32[]{:S(2)}, u32[]{:S(2)}) collective-permute-start(bf16[4,320,128]{2,1,0:T(8,128)(2,1)S(1)} %pad_maximum_fusion.6), channel_id=1, source_target_pairs={{0,4},{4,0},{8,12},{12,8},{16,20},{20,16},{24,28},{28,24},{1,5},{5... | collective-permute-start | bytes 983048 | tf_op jit(solution)/shard_map/ppermute | solution.py:488
  65.0 19.9 %collective-permute-start.12 = (bf16[8,320,128]{2,1,0:T(8,128)(2,1)}, bf16[8,320,128]{2,1,0:T(8,128)(2,1)}, u32[]{:S(2)}, u32[]{:S(2)}) collective-permute-start(bf16[8,320,128]{2,1,0:T(8,128)(2,1)} %get-tuple-element.193), channel_id=1, source_target_pairs={{0,2},{1,3},{2,0},{3,1},{4,6},{5,7},{6,4},{7,5},{8,10},{9,11},{10,... | collective-permute-start | bytes 1966088 | tf_op jit(solution)/shard_map/ppermute | solution.py:488
  70.1 27.2 %collective-permute-start.6 = (bf16[8,320,128]{2,1,0:T(8,128)(2,1)}, bf16[8,320,128]{2,1,0:T(8,128)(2,1)}, u32[]{:S(2)}, u32[]{:S(2)}) collective-permute-start(bf16[8,320,128]{2,1,0:T(8,128)(2,1)} %get-tuple-element.196), channel_id=1, source_target_pairs={{0,2},{1,3},{2,0},{3,1},{4,6},{5,7},{6,4},{7,5},{8,10},{9,11},{10,... | collective-permute-start | bytes 1966088 | tf_op jit(solution)/shard_map/ppermute | solution.py:488
  87.4 18.0 %collective-permute-start.13 = (bf16[16,320,128]{2,1,0:T(8,128)(2,1)}, bf16[16,320,128]{2,1,0:T(8,128)(2,1)S(1)}, u32[]{:S(2)}, u32[]{:S(2)}) collective-permute-start(bf16[16,320,128]{2,1,0:T(8,128)(2,1)} %get-tuple-element.181), channel_id=1, source_target_pairs={{0,1},{1,0},{2,3},{3,2},{4,5},{5,4},{6,7},{7,6},{8,9},{9,8},{10,11... | collective-permute-start | bytes 3932168 | tf_op jit(solution)/shard_map/ppermute | solution.py:488
  99.7 11.2 %collective-permute-start.7 = (bf16[16,320,128]{2,1,0:T(8,128)(2,1)}, bf16[16,320,128]{2,1,0:T(8,128)(2,1)S(1)}, u32[]{:S(2)}, u32[]{:S(2)}) collective-permute-start(bf16[16,320,128]{2,1,0:T(8,128)(2,1)} %get-tuple-element.183), channel_id=1, source_target_pairs={{0,1},{1,0},{2,3},{3,2},{4,5},{5,4},{6,7},{7,6},{8,9},{9,8},{10,11... | collective-permute-start | bytes 3932168 | tf_op jit(solution)/shard_map/ppermute | solution.py:488
  189.1 39.3 %collective-permute-start.22 = (bf16[16,320,128]{2,1,0:T(8,128)(2,1)}, bf16[16,320,128]{2,1,0:T(8,128)(2,1)}, u32[]{:S(2)}, u32[]{:S(2)}) collective-permute-start(bf16[16,320,128]{2,1,0:T(8,128)(2,1)} %slice.227), channel_id=1, source_target_pairs={{0,1},{1,0},{2,3},{3,2},{4,5},{5,4},{6,7},{7,6},{8,9},{9,8},{10,11... | collective-permute-start | bytes 3932168 | tf_op jit(solution)/shard_map/ppermute | solution.py:488
  223.3 4.3 %copy-start.16 = (f32[80,300]{1,0:T(8,128)S(1)}, f32[80,300]{1,0:T(8,128)}, u32[]{:S(2)}) copy-start(f32[80,300]{1,0:T(8,128)} %get-tuple-element.77) | copy-start | bytes 288004
  223.3 5.0 %copy-start.2 = (bf16[32,320,128]{2,1,0:T(8,128)(2,1)S(1)}, bf16[32,320,128]{2,1,0:T(8,128)(2,1)}, u32[]{:S(2)}) copy-start(bf16[32,320,128]{2,1,0:T(8,128)(2,1)} %get-tuple-element.104) | copy-start | bytes 7864324
  226.0 5.7 %collective-permute-start.16 = (bf16[16,320,128]{2,1,0:T(8,128)(2,1)}, bf16[16,320,128]{2,1,0:T(8,128)(2,1)}, u32[]{:S(2)}, u32[]{:S(2)}) collective-permute-start(bf16[16,320,128]{2,1,0:T(8,128)(2,1)} %slice.210), channel_id=1, source_target_pairs={{0,1},{1,0},{2,3},{3,2},{4,5},{5,4},{6,7},{7,6},{8,9},{9,8},{10,11... | collective-permute-start | bytes 3932168 | tf_op jit(solution)/shard_map/ppermute | solution.py:488
  228.3 3.3 %copy-start.3 = (bf16[32,320,128]{2,1,0:T(8,128)(2,1)S(1)}, bf16[32,320,128]{2,1,0:T(8,128)(2,1)}, u32[]{:S(2)}) copy-start(bf16[32,320,128]{2,1,0:T(8,128)(2,1)} %get-tuple-element.103) | copy-start | bytes 7864324
  230.2 5.1 %copy-start.6 = (f32[1280,300]{1,0:T(8,128)S(1)}, f32[1280,300]{1,0:T(8,128)}, u32[]{:S(2)}) copy-start(f32[1280,300]{1,0:T(8,128)} %get-tuple-element.101) | copy-start | bytes 4608004
  230.2 5.1 %copy-start.7 = (f32[1280,300]{1,0:T(8,128)S(1)}, f32[1280,300]{1,0:T(8,128)}, u32[]{:S(2)}) copy-start(f32[1280,300]{1,0:T(8,128)} %get-tuple-element.102) | copy-start | bytes 4608004
  230.2 18.6 %collective-permute-start.23 = (bf16[8,320,128]{2,1,0:T(8,128)(2,1)S(1)}, bf16[8,320,128]{2,1,0:T(8,128)(2,1)S(1)}, u32[]{:S(2)}, u32[]{:S(2)}) collective-permute-start(bf16[8,320,128]{2,1,0:T(8,128)(2,1)S(1)} %slice.267), channel_id=1, source_target_pairs={{0,2},{1,3},{2,0},{3,1},{4,6},{5,7},{6,4},{7,5},{8,10},{9,11},{10,... | collective-permute-start | bytes 1966088 | tf_op jit(solution)/shard_map/ppermute | solution.py:488
  233.3 2.0 copy-start
  234.3 41.1 %collective-permute-start.17 = (bf16[8,320,128]{2,1,0:T(8,128)(2,1)}, bf16[8,320,128]{2,1,0:T(8,128)(2,1)}, u32[]{:S(2)}, u32[]{:S(2)}) collective-permute-start(bf16[8,320,128]{2,1,0:T(8,128)(2,1)} %slice.255), channel_id=1, source_target_pairs={{0,2},{1,3},{2,0},{3,1},{4,6},{5,7},{6,4},{7,5},{8,10},{9,11},{10,... | collective-permute-start | bytes 1966088 | tf_op jit(solution)/shard_map/ppermute | solution.py:488
  235.5 16.7 %copy-start.9 = (bf16[1280,300]{1,0:T(8,128)(2,1)S(1)}, bf16[1280,300]{1,0:T(8,128)(2,1)}, u32[]{:S(2)}) copy-start(bf16[1280,300]{1,0:T(8,128)(2,1)} %get-tuple-element.79) | copy-start | bytes 2304004
  250.7 26.6 %collective-permute-start.24 = (bf16[4,320,128]{2,1,0:T(8,128)(2,1)}, bf16[4,320,128]{2,1,0:T(8,128)(2,1)}, u32[]{:S(2)}, u32[]{:S(2)}) collective-permute-start(bf16[4,320,128]{2,1,0:T(8,128)(2,1)} %slice.269), channel_id=1, source_target_pairs={{0,4},{4,0},{8,12},{12,8},{16,20},{20,16},{24,28},{28,24},{1,5},{5... | collective-permute-start | bytes 983048 | tf_op jit(solution)/shard_map/ppermute | solution.py:488
  261.4 14.0 %copy-start.1 = (bf16[16,320,128]{2,1,0:T(8,128)(2,1)S(1)}, bf16[16,320,128]{2,1,0:T(8,128)(2,1)}, u32[]{:S(2)}) copy-start(bf16[16,320,128]{2,1,0:T(8,128)(2,1)} %copy-done) | copy-start | bytes 3932164
  261.4 15.8 %copy-start.5 = (bf16[8,320,128]{2,1,0:T(8,128)(2,1)S(1)}, bf16[8,320,128]{2,1,0:T(8,128)(2,1)}, u32[]{:S(2)}) copy-start(bf16[8,320,128]{2,1,0:T(8,128)(2,1)} %copy-done.4) | copy-start | bytes 1966084
  276.7 9.8 %collective-permute-start.18 = (bf16[4,320,128]{2,1,0:T(8,128)(2,1)S(1)}, bf16[4,320,128]{2,1,0:T(8,128)(2,1)S(1)}, u32[]{:S(2)}, u32[]{:S(2)}) collective-permute-start(bf16[4,320,128]{2,1,0:T(8,128)(2,1)S(1)} %slice.257), channel_id=1, source_target_pairs={{0,4},{4,0},{8,12},{12,8},{16,20},{20,16},{24,28},{28,24},{1,5},{5... | collective-permute-start | bytes 983048 | tf_op jit(solution)/shard_map/ppermute | solution.py:488
  278.3 20.1 %copy-start.8 = (f32[2,36600]{1,0:T(2,128)S(1)}, f32[2,36600]{1,0:T(2,128)}, u32[]{:S(2)}) copy-start(f32[2,36600]{1,0:T(2,128)} %param.13) | copy-start | bytes 878404
  278.3 20.1 %copy-start.13 = (f32[2,36600]{1,0:T(2,128)S(1)}, f32[2,36600]{1,0:T(2,128)}, u32[]{:S(2)}) copy-start(f32[2,36600]{1,0:T(2,128)} %param.15) | copy-start | bytes 878404
  278.3 20.1 %copy-start.14 = (f32[2,36600]{1,0:T(2,128)S(1)}, f32[2,36600]{1,0:T(2,128)}, u32[]{:S(2)}) copy-start(f32[2,36600]{1,0:T(2,128)} %param.14) | copy-start | bytes 878404
  278.4 12.0 %collective-permute-start.25 = (bf16[1,320,128]{2,1,0:T(8,128)(2,1)S(1)}, bf16[1,320,128]{2,1,0:T(8,128)(2,1)S(1)}, u32[]{:S(2)}, u32[]{:S(2)}) collective-permute-start(bf16[1,320,128]{2,1,0:T(8,128)(2,1)S(1)} %get-tuple-element.188), channel_id=1, source_target_pairs={{0,8},{4,12},{8,0},{12,4},{16,24},{20,28},{24,16},{28,20},{1,9},{5... | collective-permute-start | bytes 245768 | tf_op jit(solution)/shard_map/ppermute | solution.py:488
  279.9 11.0 %collective-permute-start.27 = (bf16[1,320,128]{2,1,0:T(8,128)(2,1)S(1)}, bf16[1,320,128]{2,1,0:T(8,128)(2,1)S(1)}, u32[]{:S(2)}, u32[]{:S(2)}) collective-permute-start(bf16[1,320,128]{2,1,0:T(8,128)(2,1)S(1)} %get-tuple-element.189), channel_id=1, source_target_pairs={{0,24},{4,28},{8,16},{12,20},{16,8},{20,12},{24,0},{28,4},{1,25},{... | collective-permute-start | bytes 245768 | tf_op jit(solution)/shard_map/ppermute | solution.py:488
  282.2 8.6 %collective-permute-start.26 = (bf16[1,320,128]{2,1,0:T(8,128)(2,1)S(1)}, bf16[1,320,128]{2,1,0:T(8,128)(2,1)S(1)}, u32[]{:S(2)}, u32[]{:S(2)}) collective-permute-start(bf16[1,320,128]{2,1,0:T(8,128)(2,1)S(1)} %get-tuple-element.190), channel_id=1, source_target_pairs={{0,16},{4,20},{8,24},{12,28},{16,0},{20,4},{24,8},{28,12},{1,17},{... | collective-permute-start | bytes 245768 | tf_op jit(solution)/shard_map/ppermute | solution.py:488
  286.6 5.8 %collective-permute-start.19 = (bf16[1,320,128]{2,1,0:T(8,128)(2,1)S(1)}, bf16[1,320,128]{2,1,0:T(8,128)(2,1)S(1)}, u32[]{:S(2)}, u32[]{:S(2)}) collective-permute-start(bf16[1,320,128]{2,1,0:T(8,128)(2,1)S(1)} %get-tuple-element.185), channel_id=1, source_target_pairs={{0,8},{4,12},{8,0},{12,4},{16,24},{20,28},{24,16},{28,20},{1,9},{5... | collective-permute-start | bytes 245768 | tf_op jit(solution)/shard_map/ppermute | solution.py:488
  287.7 7.2 %collective-permute-start.21 = (bf16[1,320,128]{2,1,0:T(8,128)(2,1)S(1)}, bf16[1,320,128]{2,1,0:T(8,128)(2,1)S(1)}, u32[]{:S(2)}, u32[]{:S(2)}) collective-permute-start(bf16[1,320,128]{2,1,0:T(8,128)(2,1)S(1)} %get-tuple-element.186), channel_id=1, source_target_pairs={{0,24},{4,28},{8,16},{12,20},{16,8},{20,12},{24,0},{28,4},{1,25},{... | collective-permute-start | bytes 245768 | tf_op jit(solution)/shard_map/ppermute | solution.py:488
  290.4 7.5 %collective-permute-start.20 = (bf16[1,320,128]{2,1,0:T(8,128)(2,1)S(1)}, bf16[1,320,128]{2,1,0:T(8,128)(2,1)S(1)}, u32[]{:S(2)}, u32[]{:S(2)}) collective-permute-start(bf16[1,320,128]{2,1,0:T(8,128)(2,1)S(1)} %get-tuple-element.187), channel_id=1, source_target_pairs={{0,16},{4,20},{8,24},{12,28},{16,0},{20,4},{24,8},{28,12},{1,17},{... | collective-permute-start | bytes 245768 | tf_op jit(solution)/shard_map/ppermute | solution.py:488
  (3 other events, 4.8 us)
Sparse Core Ops, SparseCore 0:
  227.8 32.8 all-reduce.5
